TPU v7x, 256 devices: a whole 4x4x8 slice. The times are simulated.
256 devices in a mesh: af: 32 (over y, z), vert: 8 (over x, core).
Axes of the slice: x: 4, y: 4, z: 8, core: 2. Of those that a mesh axis runs over, the one named last changes fastest.
Arguments:
- recorded: float32 [256, 64, 192], P('af', 'vert'), may hold values from -170 to 170, as said below
- kernel: float32 [256, 2, 96, 512], P('af'), may hold values from -0.1875 to 0.1875
- cutoff: int32 [512], replicated, may hold values from 128 to 512, as said below
Outputs:
- solution: float32 [64, 512, 512], P('vert', 'af')
- direction: float32 [64, 512, 512], P('vert', 'af')
- left_basis_vector: float32 [256, 64, 192], P('af', 'vert')
Inputs may be any that keep to these rules, and one draw needn't show every extreme that they name: `recorded`: real parts fill the first 96 entries of the last dimension, imaginary parts the rest. `cutoff`: some receiver keeps all 512 samples and some receiver keeps a quarter of 512.
All inputs are finite; a program needn't handle non-finite values.
Results may differ from a plain program's by a relative error of at most 0.0045.
Values sent between devices are 32-bit elements; how exact they have to be, the bound alone decides.
No kernel may reach another device: no remote copies, remote signals or barrier semaphores. Data moves between devices by JAX's collectives and lax.ppermute only.
A program may use at most 64 MiB of HBM per device.

v0:
```python
import math

import jax
import jax.numpy as jnp
from jax import lax
from jax.sharding import PartitionSpec as P

FREQS = 256
SAMPLES = 512
RECV = 512
ITERS = 2


EPSILON = 1e-06


def dft_table():
    times = jnp.arange(SAMPLES, dtype=jnp.int32)
    freq_index = jnp.arange(FREQS, dtype=jnp.int32)
    phases = times[:, None] * freq_index[None, :] % SAMPLES
    angles = 2.0 * math.pi / SAMPLES * phases.astype(jnp.float32)
    scale_factor = 1.0 / math.sqrt(SAMPLES)
    return jnp.concatenate([jnp.cos(angles), -jnp.sin(angles)], axis=1) * scale_factor


def contract_forward(operand_array, weight_factors):
    return jnp.einsum(
        "pun,uln->upl", operand_array, weight_factors, precision=lax.Precision.HIGHEST
    )


def adjoint_contraction(operand_array, weight_factors):
    return jnp.einsum(
        "xug,xge->uxe", operand_array, weight_factors, precision=lax.Precision.HIGHEST
    )


def kernel_apply(spectra, kernel):
    real_part = spectra[:, 0]
    imag_part = spectra[:, 1]
    kernel_real = kernel[:, 0]
    kernel_imag = kernel[:, 1]
    out_real = contract_forward(real_part, kernel_real) - contract_forward(imag_part, kernel_imag)
    out_imag = contract_forward(real_part, kernel_imag) + contract_forward(imag_part, kernel_real)
    return jnp.concatenate([out_real, out_imag], axis=2)


def kernel_adjoint(values, kernel):
    count = kernel.shape[2]
    real_part = values[:, :, :count]
    imag_part = values[:, :, count:]
    kernel_real = kernel[:, 0]
    kernel_imag = kernel[:, 1]
    out_real = adjoint_contraction(real_part, kernel_real) + adjoint_contraction(
        imag_part, kernel_imag
    )
    out_imag = adjoint_contraction(imag_part, kernel_real) - adjoint_contraction(
        real_part, kernel_imag
    )
    return jnp.stack([out_real, out_imag], axis=1)


def transform(pieces, fourier):
    return jnp.einsum("vtr,tk->vkr", pieces, fourier, precision=lax.Precision.HIGHEST)


def inverse(pieces, fourier):
    return jnp.einsum("vkr,tk->vtr", pieces, fourier, precision=lax.Precision.HIGHEST)


def global_norm(vector):
    return jnp.sqrt(lax.psum(jnp.sum(vector * vector), ("af", "vert")) + EPSILON)


def per_device(recorded, kernel, cutoff):
    fourier = dft_table()
    group_list = lax.axis_size("af")
    position = lax.axis_index("af")
    virt_local = recorded.shape[1]
    recv_share = RECV // group_list
    time_share = SAMPLES // group_list
    sample_position = position * time_share + jnp.arange(time_share, dtype=jnp.int32)
    mask_time = (sample_position[:, None] < cutoff[None, :]).astype(jnp.float32)

    def traces_into_spectrum(values):
        spread = kernel_adjoint(values, kernel)
        arrived = lax.all_to_all(spread, "af", split_axis=3, concat_axis=2, tiled=True)
        return inverse(arrived.reshape(virt_local, 2 * FREQS, recv_share), fourier)

    def adjoint(values):
        samples = lax.all_to_all(
            traces_into_spectrum(values), "af", split_axis=1, concat_axis=2, tiled=True
        )
        return samples * mask_time

    beta_norm = global_norm(recorded)
    left_vec = recorded / beta_norm
    right_vec = adjoint(left_vec)
    alpha_norm = global_norm(right_vec)
    right_vec = right_vec / alpha_norm
    direction = right_vec
    solution = jnp.zeros_like(right_vec)
    phibar = beta_norm
    rhobar = alpha_norm
    for iteration in range(ITERS):
        forward_spectra = transform(
            lax.all_to_all(right_vec * mask_time, "af", split_axis=2, concat_axis=1, tiled=True),
            fourier,
        )
        shaped = forward_spectra.reshape(virt_local, 2, FREQS, recv_share)
        spectra_arrived = lax.all_to_all(shaped, "af", split_axis=2, concat_axis=3, tiled=True)
        left_vec = kernel_apply(spectra_arrived, kernel) - alpha_norm * left_vec
        beta_norm = global_norm(left_vec)
        left_vec = left_vec / beta_norm
        right_vec = adjoint(left_vec) - beta_norm * right_vec
        alpha_norm = global_norm(right_vec)
        right_vec = right_vec / alpha_norm
        rho_value = jnp.sqrt(rhobar * rhobar + beta_norm * beta_norm)
        cosine = rhobar / rho_value
        sine_value = beta_norm / rho_value
        theta_value = sine_value * alpha_norm
        rhobar = -cosine * alpha_norm
        phi_value = cosine * phibar
        phibar = sine_value * phibar
        solution = solution + phi_value / rho_value * direction
        direction = right_vec - theta_value / rho_value * direction
    return (solution, direction, left_vec)


def solution(mesh):
    in_specs = (P("af", "vert", None), P("af", None, None, None), P())
    out_specs = (P("vert", "af", None), P("vert", "af", None), P("af", "vert", None))
    return jax.shard_map(
        per_device, mesh=mesh, in_specs=in_specs, out_specs=out_specs, check_vma=False
    )
```

profile of v0, /device:TPU:1, one launch (start us, length us, event | category | flops | bytes accessed | tf_op | source)
XLA Modules:
  0.0 898.6 jit_solution(2503702895534353375)
XLA Ops:
  2.3 81.4 %psum.42 = f32[]{:T(128)} all-reduce(f32[]{:T(128)} %multiply_reduce_fusion.4), channel_id=1, replica_groups=mesh['af'=32,'vert'=8] {'af','vert'}, use_global_device_ids=true, to_apply=%region_1.2 | all-reduce | flops 1 | bytes 8 | tf_op jit(solution)/shard_map/psum | solution.py:72
  95.0 4.5 reshape.94
  99.4 5.7 all-to-all-start
  108.0 6.7 all-to-all-done
  122.0 4.3 copy.47
  137.5 6.4 all-to-all-start.1
  144.3 9.3 %all-to-all-done.1 = f32[32,1,2048]{2,1,0:T(1,128)} async-done(((f32[32,1,2048]{2,1,0:T(1,128)}), f32[32,1,2048]{2,1,0:T(1,128)}, u32[]{:S(2)}, u32[]{:S(2)}) %all-to-all-start.1) | async-done | bytes 262176 | tf_op jit(solution)/shard_map/all_to_all | solution.py:91
  165.6 75.8 %psum.43 = f32[]{:T(128)} all-reduce(f32[]{:T(128)} %multiply_reduce_fusion.1), channel_id=1, replica_groups=mesh['af'=32,'vert'=8] {'af','vert'}, use_global_device_ids=true, to_apply=%region_3.4 | all-reduce | flops 1 | bytes 8 | tf_op jit(solution)/shard_map/psum | solution.py:72
  242.1 4.1 copy.52
  256.0 15.8 %all_to_all.171 = f32[32,1,2048]{2,1,0:T(1,128)} all-to-all(f32[32,1,2048]{2,1,0:T(1,128)} %reshape.98), channel_id=1, replica_groups=mesh['af'=32,'vert'=8] {'af'}, dimensions={0} | all-to-all | bytes 524288 | tf_op jit(solution)/shard_map/all_to_all | solution.py:107
  277.8 4.1 copy.55
  293.8 5.0 reshape.100
  298.8 16.3 %all_to_all.172 = f32[32,1,2048]{2,1,0:T(1,128)} all-to-all(f32[32,1,2048]{2,1,0:T(1,128)} %reshape.100), channel_id=1, replica_groups=mesh['af'=32,'vert'=8] {'af'}, dimensions={0} | all-to-all | bytes 524288 | tf_op jit(solution)/shard_map/all_to_all | solution.py:111
  318.0 5.1 reshape.101
  339.0 75.7 %psum.44 = f32[]{:T(128)} all-reduce(f32[]{:T(128)} %multiply_reduce_fusion.3), channel_id=1, replica_groups=mesh['af'=32,'vert'=8] {'af','vert'}, use_global_device_ids=true, to_apply=%region_5.6 | all-reduce | flops 1 | bytes 8 | tf_op jit(solution)/shard_map/psum | solution.py:72
  420.5 4.3 copy.61
  424.9 4.5 reshape.102
  429.3 15.6 %all_to_all.173 = f32[32,1,2048]{2,1,0:T(1,128)} all-to-all(f32[32,1,2048]{2,1,0:T(1,128)} %reshape.102), channel_id=1, replica_groups=mesh['af'=32,'vert'=8] {'af'}, dimensions={0} | all-to-all | bytes 524288 | tf_op jit(solution)/shard_map/all_to_all | solution.py:87
  448.0 4.5 reshape.103
  452.5 4.3 copy.63
  468.7 16.2 %all_to_all.174 = f32[32,1,2048]{2,1,0:T(1,128)} all-to-all(f32[32,1,2048]{2,1,0:T(1,128)} %reshape.104), channel_id=1, replica_groups=mesh['af'=32,'vert'=8] {'af'}, dimensions={0} | all-to-all | bytes 524288 | tf_op jit(solution)/shard_map/all_to_all | solution.py:91
  497.6 75.3 %psum.45 = f32[]{:T(128)} all-reduce(f32[]{:T(128)} %multiply_reduce_fusion), channel_id=1, replica_groups=mesh['af'=32,'vert'=8] {'af','vert'}, use_global_device_ids=true, to_apply=%region_7.8 | all-reduce | flops 1 | bytes 8 | tf_op jit(solution)/shard_map/psum | solution.py:72
  573.6 4.1 copy.67
  589.0 15.9 %all_to_all.175 = f32[32,1,2048]{2,1,0:T(1,128)} all-to-all(f32[32,1,2048]{2,1,0:T(1,128)} %reshape.106), channel_id=1, replica_groups=mesh['af'=32,'vert'=8] {'af'}, dimensions={0} | all-to-all | bytes 524288 | tf_op jit(solution)/shard_map/all_to_all | solution.py:107
  626.9 5.0 reshape.108
  631.9 16.4 %all_to_all.176 = f32[32,1,2048]{2,1,0:T(1,128)} all-to-all(f32[32,1,2048]{2,1,0:T(1,128)} %reshape.108), channel_id=1, replica_groups=mesh['af'=32,'vert'=8] {'af'}, dimensions={0} | all-to-all | bytes 524288 | tf_op jit(solution)/shard_map/all_to_all | solution.py:111
  651.3 5.1 reshape.109
  673.0 75.5 %psum.46 = f32[]{:T(128)} all-reduce(f32[]{:T(128)} %multiply_reduce_fusion.2), channel_id=1, replica_groups=mesh['af'=32,'vert'=8] {'af','vert'}, use_global_device_ids=true, to_apply=%region_9.10 | all-reduce | flops 1 | bytes 8 | tf_op jit(solution)/shard_map/psum | solution.py:72
  760.9 15.3 %all_to_all.177 = f32[32,1,2048]{2,1,0:T(1,128)S(1)} all-to-all(f32[32,1,2048]{2,1,0:T(1,128)S(1)} %reshape.110), channel_id=1, replica_groups=mesh['af'=32,'vert'=8] {'af'}, dimensions={0} | all-to-all | bytes 524288 | tf_op jit(solution)/shard_map/all_to_all | solution.py:87
  790.4 6.5 all-to-all-start.9
  797.3 9.3 %all-to-all-done.9 = f32[32,1,2048]{2,1,0:T(1,128)S(1)} async-done(((f32[32,1,2048]{2,1,0:T(1,128)}), f32[32,1,2048]{2,1,0:T(1,128)S(1)}, u32[]{:S(2)}, u32[]{:S(2)}) %all-to-all-start.9) | async-done | bytes 262176 | tf_op jit(solution)/shard_map/all_to_all | solution.py:91
  821.3 75.4 %psum.47 = f32[]{:T(128)} all-reduce(f32[]{:T(128)} %fusion.2), channel_id=1, replica_groups=mesh['af'=32,'vert'=8] {'af','vert'}, use_global_device_ids=true, to_apply=%region_11.12 | all-reduce | flops 1 | bytes 8 | tf_op jit(solution)/shard_map/psum | solution.py:72
  (143 shorter events, 219.3 us)
Async XLA Ops:
  0.6 89.1 %copy-start = (f32[8,2,96,512]{3,2,1,0:T(8,128)S(1)}, f32[8,2,96,512]{3,2,1,0:T(8,128)}, u32[]{:S(2)}) copy-start(f32[8,2,96,512]{3,2,1,0:T(8,128)} %param.4) | copy-start | bytes 9437188
  99.4 15.3 %all-to-all-start = ((f32[32,1,2048]{2,1,0:T(1,128)}), f32[32,1,2048]{2,1,0:T(1,128)S(1)}, u32[]{:S(2)}, u32[]{:S(2)}) async-start(f32[32,1,2048]{2,1,0:T(1,128)} %reshape.94), calls=%async_computation | async-start | bytes 524288 | tf_op jit(solution)/shard_map/all_to_all | solution.py:87
  114.8 0.7 copy-start.10
  131.6 12.4 %copy-start.20 = (s32[512]{0:T(512)S(1)}, s32[512]{0:T(512)}, u32[]{:S(2)}) copy-start(s32[512]{0:T(512)} %param.5) | copy-start | bytes 6148
  137.5 16.1 %all-to-all-start.1 = ((f32[32,1,2048]{2,1,0:T(1,128)}), f32[32,1,2048]{2,1,0:T(1,128)}, u32[]{:S(2)}, u32[]{:S(2)}) async-start(f32[32,1,2048]{2,1,0:T(1,128)} %reshape.96), calls=%async_computation.1 | async-start | bytes 524288 | tf_op jit(solution)/shard_map/all_to_all | solution.py:91
  144.3 18.5 %copy-start.5 = (f32[16,32,16]{0,1,2:T(8,128)}, f32[16,32,16]{0,1,2:T(8,128)S(1)}, u32[]{:S(2)}) copy-start(f32[16,32,16]{0,1,2:T(8,128)S(1)} %compare_convert_fusion) | copy-start | bytes 98308
  165.6 83.7 %copy-start.13 = (f32[16,512]{1,0:T(8,128)}, f32[16,512]{1,0:T(8,128)S(1)}, u32[]{:S(2)}) copy-start(f32[16,512]{1,0:T(8,128)S(1)} %compare_convert_fusion.1) | copy-start | bytes 98308
  330.8 4.7 copy-start.8
  335.5 2.8 copy-start.11
  336.9 78.5 %copy-start.17 = (f32[8,8,96]{2,1,0:T(8,128)}, f32[8,8,96]{2,1,0:T(8,128)S(1)}, u32[]{:S(2)}) copy-start(f32[8,8,96]{2,1,0:T(8,128)S(1)} %fusion.83) | copy-start | bytes 73732
  338.3 77.1 %copy-start.19 = (f32[8,8,96]{2,1,0:T(8,128)}, f32[8,8,96]{2,1,0:T(8,128)S(1)}, u32[]{:S(2)}) copy-start(f32[8,8,96]{2,1,0:T(8,128)S(1)} %fusion.80) | copy-start | bytes 73732
  577.7 3.7 copy-start.14
  664.1 4.7 copy-start.9
  670.2 1.4 copy-start.16
  671.6 0.6 copy-start.18
  750.0 2.6 copy-start.12
  784.7 1.3 copy-start.2
  784.7 1.3 copy-start.3
  790.4 16.1 %all-to-all-start.9 = ((f32[32,1,2048]{2,1,0:T(1,128)}), f32[32,1,2048]{2,1,0:T(1,128)S(1)}, u32[]{:S(2)}, u32[]{:S(2)}) async-start(f32[32,1,2048]{2,1,0:T(1,128)} %reshape.112), calls=%async_computation.9 | async-start | bytes 524288 | tf_op jit(solution)/shard_map/all_to_all | solution.py:91
  808.6 2.6 copy-start.4
  811.2 3.3 copy-start.1
  811.2 3.3 copy-start.6
  818.2 79.2 %copy-start.7 = (f32[8,16,512]{2,1,0:T(8,128)S(1)}, f32[8,16,512]{2,1,0:T(8,128)}, u32[]{:S(2)}) copy-start(f32[8,16,512]{2,1,0:T(8,128)} %all_to_all.145) | copy-start | bytes 786436
  818.2 79.2 %copy-start.15 = (f32[16,512]{1,0:T(8,128)S(1)}, f32[16,512]{1,0:T(8,128)}, u32[]{:S(2)}) copy-start(f32[16,512]{1,0:T(8,128)} %copy-done.13) | copy-start | bytes 98308
where the time goes:
time: 907 us; the launch traced here: 899 us
  blocking collectives  571 us (63%)
  local copies, waits for them, and re-layouts  188 us (21%)
  other arithmetic  48.4 us (5%)
  matrix products  42.1 us (5%)
  waiting for transfers between devices  25.3 us (3%)
  starting transfers between devices  18.6 us (2%)
    psum x6, blocking collectives, global_norm(): lax.psum(jnp.sum(vector * vector), ('af', 'vert')) + EPSILON  459 us
    unnamed x62, local copies, waits for them, and re-layouts  72.4 us
    all_to_all x2, blocking collectives, per_device(): lax.all_to_all(shaped, 'af', split_axis=2, concat_axis=3, tiled=True)  32.7 us
    all_to_all x2, blocking collectives, per_device(): lax.all_to_all(right_vec * mask_time, 'af', split_axis=2, concat_axis=1,...  31.7 us
    all_to_all x2, blocking collectives, traces_into_spectrum(): lax.all_to_all(spread, 'af', split_axis=3, concat_axis=2, tiled=True)  31 us
    all_to_all x9, local copies, waits for them, and re-layouts, adjoint(): lax.all_to_all(traces_into_spectrum(values), 'af', split_axis=1, concat_a...  30.4 us
    all_to_all x2, waiting for transfers between devices, adjoint(): lax.all_to_all(traces_into_spectrum(values), 'af', split_axis=1, concat_a...  18.6 us
  transfers between devices with their start and end apart: 3, of which 3 were waited for; matrix products, arithmetic and copies ran while one was open for 0% of the time, Pallas kernels for 0%

commit v1 on v0

v1 whole, which is shorter than its diff:
```python
import math

import jax
import jax.numpy as jnp
import numpy as np
from jax import lax
from jax.experimental import pallas as pl
from jax.experimental.pallas import tpu as pltpu
from jax.sharding import PartitionSpec as P

FREQS = 256
SAMPLES = 512
RECV = 512
SRCS = 96
EPSILON = 1e-06
F32 = jnp.float32
BF16 = jnp.bfloat16

AF = 32
VERT = 8
FB = FREQS // AF
VB = 8
QB = RECV // 128
KB = 2 * FB
MSG = KB + 1
TB = SAMPLES // AF
LAST = 3 * TB + 1
VMEM = 48 * 1024 * 1024


def dft_tables():
    times = np.arange(SAMPLES)
    freqs = np.arange(FREQS)
    angles = 2.0 * math.pi / SAMPLES * ((times[:, None] * freqs[None, :]) % SAMPLES)
    scale = 1.0 / math.sqrt(SAMPLES)
    table = np.stack([np.cos(angles), -np.sin(angles)], axis=2) * scale
    table = table.reshape(SAMPLES, 2 * FREQS).astype(np.float32)
    out = []
    for t in (table, np.ascontiguousarray(table.T)):
        hi = t.astype(jnp.bfloat16)
        out += [hi, (t - hi.astype(np.float32)).astype(jnp.bfloat16)]
    return out


def split(x):
    hi = x.astype(BF16)
    return hi, (x - hi.astype(F32)).astype(BF16)


def dot(a, b):
    return lax.dot_general(a, b, (((1,), (0,)), ((), ())), preferred_element_type=F32)


def dot_nt(a, b):
    return lax.dot_general(a, b, (((1,), (1,)), ((), ())), preferred_element_type=F32)


def turned(x, sign):
    return jnp.concatenate([sign * x[:, SRCS:], -sign * x[:, :SRCS]], axis=1)


def kernel_adjoint(u, khi, klo):
    hi, lo = split(jnp.concatenate([u, turned(u, 1.0)], axis=0))
    both = dot(jnp.concatenate([hi, lo], axis=0), khi)
    return both[: 2 * VB] + both[2 * VB :] + dot(hi, klo)


def kernel_forward(x, khi, klo):
    hi, lo = split(x)
    both = dot_nt(jnp.concatenate([hi, lo], axis=0), khi)
    y = both[: 2 * VB] + both[2 * VB :] + dot_nt(hi, klo)
    return y[:VB] + turned(y[VB:], -1.0)


def ratio(a, b):
    return jnp.where(b > 0, a / jnp.where(b > 0, b, 1.0), 0.0)


def arrived_sum(recv, pitch):
    rows = recv[pl.ds(pitch - 1, AF, stride=pitch), :]
    return jnp.broadcast_to(jnp.sum(rows, keepdims=True), (1, 128))


def lane_zero(total):
    lane = lax.broadcasted_iota(jnp.int32, (1, 128), 1)
    return jnp.where(lane == 0, jnp.broadcast_to(total, (1, 128)), 0.0)


def put_spectra(msg, f, z):
    for c in range(2):
        for q in range(QB):
            msg[pl.ds(q * MSG + 2 * f + c, VB, stride=QB * MSG), :] = z[
                c * VB : (c + 1) * VB, q * 128 : (q + 1) * 128
            ]


def put_partial(msg, row, pitch):
    for d in range(AF):
        msg[pl.ds(d * pitch + pitch - 1, 1), :] = row


def first_kernel(u_ref, k_ref, msg, khi_ref, klo_ref):
    square = jnp.zeros((VB, 2 * SRCS), F32)
    for f in range(FB):
        u = u_ref[f]
        square += u * u
        khi, klo = split(k_ref[f])
        khi_ref[f] = khi
        klo_ref[f] = klo
        put_spectra(msg, f, kernel_adjoint(u, khi, klo))
    put_partial(msg, lane_zero(jnp.sum(square, keepdims=True)), MSG)


def data_kernel(order, recv, khi_ref, klo_ref, before_ref, stats, msg, q_ref, stats_out):
    total = arrived_sum(recv, MSG)
    stats_out[...] = stats[...]
    stats_out[pl.ds(order, 1), :] = total
    coefficient = ratio(total, stats[pl.ds(order - 1, 1), :])[:, :1]
    square = jnp.zeros((VB, 2 * SRCS), F32)
    for f in range(FB):
        khi, klo = khi_ref[f], klo_ref[f]
        x = jnp.concatenate(
            [
                jnp.concatenate(
                    [
                        recv[pl.ds(q * MSG + 2 * f + c, VB, stride=QB * MSG), :]
                        for q in range(QB)
                    ],
                    axis=1,
                )
                for c in range(2)
            ],
            axis=0,
        )
        u = kernel_forward(x, khi, klo) - coefficient * before_ref[f]
        q_ref[f] = u
        square += u * u
        put_spectra(msg, f, kernel_adjoint(u, khi, klo))
    put_partial(msg, lane_zero(jnp.sum(square, keepdims=True)), MSG)


def table_apply(hi_ref, lo_ref, x):
    hi, lo = split(x)
    both = dot(hi_ref[...], jnp.concatenate([hi, lo], axis=1))
    return both[:, :128] + both[:, 128:] + dot(lo_ref[...], hi)


def model_kernel(order, last, *refs):
    refs = list(refs)
    recv, cut_ref, inv_hi, inv_lo = refs[:4]
    refs = refs[4:]
    if not last:
        fwd_hi, fwd_lo = refs[:2]
        refs = refs[2:]
    if order > 0:
        stats = refs.pop(0)
        earlier = [refs.pop(0) for _ in range(order // 2)]
    total = arrived_sum(recv, MSG)
    spectra = jnp.concatenate([recv[pl.ds(p * MSG, KB), :] for p in range(AF)], axis=0)
    s = table_apply(inv_hi, inv_lo, spectra)
    if order > 0:
        s = s - ratio(total, stats[pl.ds(order - 1, 1), :]) * earlier[-1][...]
    keep = lax.broadcasted_iota(jnp.int32, (SAMPLES, 128), 0) < cut_ref[...]
    s = jnp.where(keep, s, 0.0)
    partial = jnp.sum(s * s, axis=0, keepdims=True)
    if last:
        msg, stats_out = refs
    else:
        msg, s_ref, stats_out = refs
        s_ref[...] = s
    stats_out[...] = stats[...] if order > 0 else jnp.zeros((8, 128), F32)
    stats_out[pl.ds(order, 1), :] = total
    if last:
        for j, value in enumerate([e[...] for e in earlier] + [s]):
            for p in range(AF):
                msg[pl.ds(p * LAST + j * TB, TB), :] = value[p * TB : (p + 1) * TB]
        put_partial(msg, partial, LAST)
    else:
        out = table_apply(fwd_hi, fwd_lo, s)
        for p in range(AF):
            msg[pl.ds(p * MSG, KB), :] = out[p * KB : (p + 1) * KB]
        put_partial(msg, partial, MSG)


def stats_kernel(recv, stats, out):
    total = arrived_sum(recv, LAST)
    row = lax.broadcasted_iota(jnp.int32, (8, 128), 0)
    mine = jnp.where(row == 5, total, stats[...])
    for g in range(VERT):
        out[pl.ds(8 * g, 8), :] = mine


def last_kernel(group_ref, recv, gathered, q0_ref, q1_ref, q2_ref, sol_ref, dir_ref, left_ref, rows):
    n0, m1, n1, m2, n2, m3 = [gathered[pl.ds(j, VERT, stride=8), :] for j in range(6)]

    def norm(x):
        return jnp.sqrt(jnp.sum(x, axis=0, keepdims=True) + EPSILON)

    theta, kappa, lam, mu = ratio(m1, n0), ratio(n1, m1), ratio(m2, n1), ratio(n2, m2)
    beta0 = norm(n0)
    alpha1 = norm(m1 / (beta0 * beta0))
    e = 1.0 / (beta0 * alpha1)
    d = e * theta - alpha1 / beta0
    beta1 = norm(e * e * n1 + d * d * n0)
    f1 = e / beta1
    f0 = d / beta1
    h = f1 * kappa + f0 - beta1 * e
    alpha2 = norm(f1 * f1 * m2 + h * h * m1)
    g2 = f1 / alpha2
    g1 = h / alpha2
    rho1 = jnp.sqrt(alpha1 * alpha1 + beta1 * beta1)
    cos1, sin1 = alpha1 / rho1, beta1 / rho1
    theta1 = sin1 * alpha2
    rhobar = -cos1 * alpha2
    phi1, phibar = cos1 * beta0, sin1 * beta0
    w2 = g2
    w1 = g1 - theta1 / rho1 * e
    c2 = g2
    c1 = g2 * lam + g1 - alpha2 * f1
    c0 = g1 * theta - alpha2 * f0
    beta2 = norm(c2 * c2 * n2 + c1 * c1 * n1 + c0 * c0 * n0)
    c2, c1, c0 = c2 / beta2, c1 / beta2, c0 / beta2
    z3 = c2
    z2 = c2 * mu + c1 - beta2 * g2
    z1 = c1 * kappa + c0 - beta2 * g1
    alpha3 = norm(z3 * z3 * m3 + z2 * z2 * m2 + z1 * z1 * m1)
    rho2 = jnp.sqrt(rhobar * rhobar + beta2 * beta2)
    cos2, sin2 = rhobar / rho2, beta2 / rho2
    step2 = cos2 * phibar / rho2
    turn2 = sin2 * alpha3 / rho2
    x1 = phi1 / rho1 * e + step2 * w1
    x2 = step2 * w2
    y1 = z1 / alpha3 - turn2 * w1
    y2 = z2 / alpha3 - turn2 * w2
    y3 = z3 / alpha3
    for j, value in enumerate((x1, x2, y1, y2, y3, c0, c1, c2)):
        rows[pl.ds(8 * j, 8), :] = jnp.broadcast_to(value, (VERT, 128))
    group = group_ref[0]
    x1, x2, y1, y2, y3, c0, c1, c2 = [rows[pl.ds(8 * j + group, 1), :] for j in range(8)]
    for v in range(VB):
        for q in range(QB):
            at = (v * QB + q) * LAST
            s1, s2, s3 = [recv[pl.ds(at + j * TB, TB), :] for j in range(3)]
            sol_ref[v, :, q * 128 : (q + 1) * 128] = x1 * s1 + x2 * s2
            dir_ref[v, :, q * 128 : (q + 1) * 128] = y1 * s1 + y2 * s2 + y3 * s3
    c0, c1, c2 = c0[:, :1], c1[:, :1], c2[:, :1]
    for f in range(FB):
        left_ref[f] = c0 * q0_ref[f] + c1 * q1_ref[f] + c2 * q2_ref[f]


def call(body, outs, *operands, scratch=(), smem=0):
    vmem = pl.BlockSpec(memory_space=pltpu.VMEM)
    return pl.pallas_call(
        body,
        out_shape=[jax.ShapeDtypeStruct(s, t) for s, t in outs],
        in_specs=[pl.BlockSpec(memory_space=pltpu.SMEM)] * smem + [vmem] * (len(operands) - smem),
        out_specs=[vmem] * len(outs),
        scratch_shapes=list(scratch),
        compiler_params=pltpu.CompilerParams(vmem_limit_bytes=VMEM),
    )(*operands)


def exchange(message):
    return lax.all_to_all(message, "af", split_axis=0, concat_axis=0, tiled=True)


def per_device(recorded, kernel, cutoff):
    import functools

    inv_hi, inv_lo, fwd_hi, fwd_lo = [jnp.asarray(t) for t in dft_tables()]
    place = lax.axis_index("af")
    cut = lax.dynamic_slice(cutoff.reshape(QB, 128), (place % QB, 0), (1, 128))
    kernel = kernel.reshape(FB, 2 * SRCS, RECV)
    message = ((AF * MSG, 128), F32)
    data = ((FB, VB, 2 * SRCS), F32)
    model = ((SAMPLES, 128), F32)
    stat = ((8, 128), F32)
    wide = ((FB, 2 * SRCS, RECV), BF16)

    msg, khi, klo = call(first_kernel, [message, wide, wide], recorded, kernel)
    msg, s1, stats = call(
        functools.partial(model_kernel, 0, False),
        [message, model, stat],
        exchange(msg), cut, inv_hi, inv_lo, fwd_hi, fwd_lo,
    )
    msg, q1, stats = call(
        functools.partial(data_kernel, 1),
        [message, data, stat],
        exchange(msg), khi, klo, recorded, stats,
    )
    msg, s2, stats = call(
        functools.partial(model_kernel, 2, False),
        [message, model, stat],
        exchange(msg), cut, inv_hi, inv_lo, fwd_hi, fwd_lo, stats, s1,
    )
    msg, q2, stats = call(
        functools.partial(data_kernel, 3),
        [message, data, stat],
        exchange(msg), khi, klo, q1, stats,
    )
    msg, stats = call(
        functools.partial(model_kernel, 4, True),
        [((AF * LAST, 128), F32), stat],
        exchange(msg), cut, inv_hi, inv_lo, stats, s1, s2,
    )
    arrived = exchange(msg)
    [stats] = call(stats_kernel, [((VERT * 8, 128), F32)], arrived, stats)
    gathered = lax.all_to_all(stats, "vert", split_axis=0, concat_axis=0, tiled=True)
    group = lax.axis_index("vert").astype(jnp.int32).reshape(1)
    out = ((VB, TB, RECV), F32)
    return tuple(
        call(
            last_kernel,
            [out, out, data],
            group, arrived, gathered, recorded, q1, q2,
            scratch=[pltpu.VMEM((64, 128), F32)],
            smem=1,
        )
    )


def solution(mesh):
    in_specs = (P("af", "vert", None), P("af", None, None, None), P())
    out_specs = (P("vert", "af", None), P("vert", "af", None), P("af", "vert", None))
    return jax.shard_map(
        per_device, mesh=mesh, in_specs=in_specs, out_specs=out_specs, check_vma=False
    )
```

time: 907 us -> 180 us (0.20)
  blocking collectives: 571 us -> 92.5 us
  local copies, waits for them, and re-layouts: 188 us -> 27.8 us
  other arithmetic: 48.4 us -> 0 us
  matrix products: 42.1 us -> 0 us
  Pallas kernels: 0 us -> 15.6 us
    psum x6 -> x0, blocking collectives: 459 us -> none  [global_norm(): lax.psum(jnp.sum(vector * vector), ('af', 'vert')) + EPSILON]
    all_to_all x23 -> x12, local copies, waits for them, and re-layouts: 74.1 us -> 11.3 us  [exchange(): lax.all_to_all(message, 'af', split_axis=0, concat_axis=0, tiled=True)]
    unnamed x62 -> x54, local copies, waits for them, and re-layouts: 72.4 us -> 16.5 us
    dot_general x20 -> x0, matrix products: 28.1 us -> none  [the longest x8 15 us: contract_forward(): jnp.einsum('pun,uln->upl', operand_array, weight_factors, precision=lax.P...]
    all_to_all x10 -> x0, other arithmetic: 25.6 us -> none  [the longest x3 7.22 us: adjoint(): lax.all_to_all(traces_into_spectrum(values), 'af', split_axis=1, concat_a...]
    all_to_all x7 -> x5, blocking collectives: 112 us -> 92.5 us  [exchange(): lax.all_to_all(message, 'af', split_axis=0, concat_axis=0, tiled=True)]
    reshape x7 -> x0, local copies, waits for them, and re-layouts: 17.4 us -> none  [the longest x4 11.1 us: per_device(): shaped = forward_spectra.reshape(virt_local, 2, FREQS, recv_share)]
    pallas_call x0 -> x8, Pallas kernels: none -> 15.6 us  [call(): pl.pallas_call(body, out_shape=[jax.ShapeDtypeStruct(s, t) for s, t in ou...]
  transfers between devices with their start and end apart: 3 -> 2, of which waited for: 3 -> 2; matrix products, arithmetic and copies ran while one was open for 0% -> 0% of each run, Pallas kernels for 0% -> 0%
where the time goes in v1:
time: 180 us; the launch traced here: 178 us
  blocking collectives  92.5 us (51%)
  local copies, waits for them, and re-layouts  27.8 us (15%)
  starting transfers between devices  25.3 us (14%)
  waiting for transfers between devices  16.3 us (9%)
  Pallas kernels  15.6 us (9%)
    all_to_all x5, blocking collectives, exchange(): lax.all_to_all(message, 'af', split_axis=0, concat_axis=0, tiled=True)  92.5 us
    unnamed x54, local copies, waits for them, and re-layouts  16.5 us
    pallas_call x8, Pallas kernels, call(): pl.pallas_call(body, out_shape=[jax.ShapeDtypeStruct(s, t) for s, t in ou...  15.6 us
    all_to_all x1, starting transfers between devices, per_device(): lax.all_to_all(stats, 'vert', split_axis=0, concat_axis=0, tiled=True)  13.2 us
    all_to_all x1, starting transfers between devices, exchange(): lax.all_to_all(message, 'af', split_axis=0, concat_axis=0, tiled=True)  12.1 us
    all_to_all x1, waiting for transfers between devices, exchange(): lax.all_to_all(message, 'af', split_axis=0, concat_axis=0, tiled=True)  11.6 us
    all_to_all x12, local copies, waits for them, and re-layouts, exchange(): lax.all_to_all(message, 'af', split_axis=0, concat_axis=0, tiled=True)  11.3 us
    all_to_all x1, waiting for transfers between devices, per_device(): lax.all_to_all(stats, 'vert', split_axis=0, concat_axis=0, tiled=True)  4.72 us
  transfers between devices with their start and end apart: 2, of which 2 were waited for; matrix products, arithmetic and copies ran while one was open for 0% of the time, Pallas kernels for 0%

profile of v1, /device:TPU:1, one launch (start us, length us, event | category | flops | bytes accessed | tf_op | source)
XLA Modules:
  0.0 178.4 jit_solution(12181860602538990100)
XLA Ops:
  0.7 0.8 copy-done.14
  1.5 2.8 %shard_map.94 = (f32[544,128]{1,0:T(8,128)S(1)}, bf16[8,192,512]{2,1,0:T(8,128)(2,1)S(1)}, bf16[8,192,512]{2,1,0:T(8,128)(2,1)S(1)}) custom-call(f32[8,8,192]{2,1,0:T(8,128)S(1)} %copy-done.14, f32[8,192,512]{2,1,0:T(8,128)} %bitcast.7), custom_call_target="tpu_custom_call" | custom-call | tf_op jit(solution)/shard_map/pallas_call | solution.py:253
  5.1 12.1 %all-to-all-start = ((f32[32,17,128]{2,1,0:T(8,128)}), f32[32,17,128]{2,1,0:T(8,128)}, u32[]{:S(2)}, u32[]{:S(2)}) async-start(f32[32,17,128]{2,1,0:T(8,128)} %all_to_all.49), calls=%async_computation | async-start | bytes 786432 | tf_op jit(solution)/shard_map/all_to_all | solution.py:264
  17.3 11.6 %all-to-all-done = f32[32,17,128]{2,1,0:T(8,128)} async-done(((f32[32,17,128]{2,1,0:T(8,128)}), f32[32,17,128]{2,1,0:T(8,128)}, u32[]{:S(2)}, u32[]{:S(2)}) %all-to-all-start) | async-done | bytes 278560 | tf_op jit(solution)/shard_map/all_to_all | solution.py:264
  28.9 1.0 all_to_all.51.refs_0_
  29.9 1.0 copy-done.1
  30.9 1.0 copy-done.4
  32.0 1.0 copy-done.7
  33.0 1.0 copy-done.9
  36.3 1.8 all_to_all.52
  38.0 18.3 %all_to_all.77 = f32[32,17,128]{2,1,0:T(8,128)} all-to-all(f32[32,17,128]{2,1,0:T(8,128)} %all_to_all.52), channel_id=1, replica_groups=mesh['af'=32,'vert'=8] {'af'}, dimensions={0} | all-to-all | bytes 557056 | tf_op jit(solution)/shard_map/all_to_all | solution.py:264
  56.3 1.0 all_to_all.54.recv
  57.4 4.5 %shard_map.96 = (f32[544,128]{1,0:T(8,128)S(1)}, f32[8,8,192]{2,1,0:T(8,128)S(1)}, f32[8,128]{1,0:T(8,128)S(1)}) custom-call(f32[544,128]{1,0:T(8,128)S(1)} %all_to_all.54.recv, bf16[8,192,512]{2,1,0:T(8,128)(2,1)S(1)} %get-tuple-element.22.khi_ref, bf16[8,192,512]{2,1,0:T(8,128)(2,1)S(1)} %get-tuple-element.23.klo_ref, f32[8,8,192]{2,1,0:T(8,128)S(1)} %copy-done.15, ...), custom_call_target="tpu_custom_call" | custom-call | tf_op jit(solution)/shard_map/pallas_call | solution.py:253
  63.2 1.7 all_to_all.55
  64.9 17.8 %all_to_all.78 = f32[32,17,128]{2,1,0:T(8,128)} all-to-all(f32[32,17,128]{2,1,0:T(8,128)} %all_to_all.55), channel_id=1, replica_groups=mesh['af'=32,'vert'=8] {'af'}, dimensions={0} | all-to-all | bytes 557056 | tf_op jit(solution)/shard_map/all_to_all | solution.py:264
  82.7 1.0 all_to_all.57.refs_0_
  83.8 1.0 copy-done.2
  84.8 1.0 copy-done.5
  85.8 1.0 copy-done.8
  86.9 1.0 copy-done.10
  87.9 0.9 copy-done.12
  91.1 1.7 all_to_all.58
  92.8 17.4 %all_to_all.79 = f32[32,17,128]{2,1,0:T(8,128)} all-to-all(f32[32,17,128]{2,1,0:T(8,128)} %all_to_all.58), channel_id=1, replica_groups=mesh['af'=32,'vert'=8] {'af'}, dimensions={0} | all-to-all | bytes 557056 | tf_op jit(solution)/shard_map/all_to_all | solution.py:264
  110.2 1.0 all_to_all.60.recv
  111.3 0.8 copy-done.21
  112.1 4.5 %shard_map.98 = (f32[544,128]{1,0:T(8,128)S(1)}, f32[8,8,192]{2,1,0:T(8,128)S(1)}, f32[8,128]{1,0:T(8,128)S(1)}) custom-call(f32[544,128]{1,0:T(8,128)S(1)} %all_to_all.60.recv, bf16[8,192,512]{2,1,0:T(8,128)(2,1)S(1)} %get-tuple-element.22.khi_ref, bf16[8,192,512]{2,1,0:T(8,128)(2,1)S(1)} %get-tuple-element.23.klo_ref, f32[8,8,192]{2,1,0:T(8,128)S(1)} %copy-done.21, ...), custom_call_target="tpu_custom_call" | custom-call | tf_op jit(solution)/shard_map/pallas_call | solution.py:253
  117.9 1.1 all_to_all.61
  119.0 16.3 %all_to_all.80 = f32[32,17,128]{2,1,0:T(8,128)S(1)} all-to-all(f32[32,17,128]{2,1,0:T(8,128)S(1)} %all_to_all.61), channel_id=1, replica_groups=mesh['af'=32,'vert'=8] {'af'}, dimensions={0} | all-to-all | bytes 557056 | tf_op jit(solution)/shard_map/all_to_all | solution.py:264
  135.9 22.7 %all_to_all.81 = f32[32,49,128]{2,1,0:T(8,128)S(1)} all-to-all(f32[32,49,128]{2,1,0:T(8,128)S(1)} %all_to_all.64), channel_id=1, replica_groups=mesh['af'=32,'vert'=8] {'af'}, dimensions={0} | all-to-all | bytes 1605632 | tf_op jit(solution)/shard_map/all_to_all | solution.py:264
  159.4 13.2 %all-to-all-start.6 = ((f32[8,8,128]{2,1,0:T(8,128)}), f32[8,8,128]{2,1,0:T(8,128)S(1)}, u32[]{:S(2)}, u32[]{:S(2)}) async-start(f32[8,8,128]{2,1,0:T(8,128)} %bitcast.3), calls=%async_computation.6 | async-start | bytes 65536 | tf_op jit(solution)/shard_map/all_to_all | solution.py:308
  172.6 4.7 %all-to-all-done.6 = f32[8,8,128]{2,1,0:T(8,128)S(1)} async-done(((f32[8,8,128]{2,1,0:T(8,128)}), f32[8,8,128]{2,1,0:T(8,128)S(1)}, u32[]{:S(2)}, u32[]{:S(2)}) %all-to-all-start.6) | async-done | bytes 32800 | tf_op jit(solution)/shard_map/all_to_all | solution.py:308
  177.3 1.1 shard_map.101
  (52 shorter events, 9.3 us)
Async XLA Ops:
  0.6 16.6 %copy-start = (s32[512]{0:T(512)S(1)}, s32[512]{0:T(512)}, u32[]{:S(2)}) copy-start(s32[512]{0:T(512)} %param.9) | copy-start | bytes 6148
  0.6 0.8 copy-start.14
  5.1 23.8 %all-to-all-start = ((f32[32,17,128]{2,1,0:T(8,128)}), f32[32,17,128]{2,1,0:T(8,128)}, u32[]{:S(2)}, u32[]{:S(2)}) async-start(f32[32,17,128]{2,1,0:T(8,128)} %all_to_all.49), calls=%async_computation | async-start | bytes 786432 | tf_op jit(solution)/shard_map/all_to_all | solution.py:264
  29.9 1.0 copy-start.1
  30.9 1.0 copy-start.4
  32.0 1.0 copy-start.7
  33.0 1.0 copy-start.9
  34.9 0.7 copy-start.11
  35.6 0.7 copy-start.19
  36.3 21.1 %copy-start.15 = (f32[8,8,192]{2,1,0:T(8,128)S(1)}, f32[8,8,192]{2,1,0:T(8,128)}, u32[]{:S(2)}) copy-start(f32[8,8,192]{2,1,0:T(8,128)} %q0_ref.1) | copy-start | bytes 147460
  61.8 0.7 copy-start.18
  62.6 0.6 copy-start.20
  83.8 1.0 copy-start.2
  84.8 1.0 copy-start.5
  85.8 1.0 copy-start.8
  86.9 1.0 copy-start.10
  87.9 0.9 copy-start.12
  89.7 0.7 copy-start.16
  90.4 0.7 copy-start.23
  111.3 0.8 copy-start.21
  116.6 0.7 copy-start.17
  117.3 0.6 copy-start.25
  117.9 17.4 %copy-start.3 = (bf16[512,512]{1,0:T(8,128)(2,1)S(1)}, bf16[512,512]{1,0:T(8,128)(2,1)}, u32[]{:S(2)}) copy-start(bf16[512,512]{1,0:T(8,128)(2,1)} %constant.32.clone.refs_3_) | copy-start | bytes 1572868
  117.9 17.4 %copy-start.6 = (bf16[512,512]{1,0:T(8,128)(2,1)S(1)}, bf16[512,512]{1,0:T(8,128)(2,1)}, u32[]{:S(2)}) copy-start(bf16[512,512]{1,0:T(8,128)(2,1)} %constant.31.clone.refs_2_) | copy-start | bytes 1572868
  117.9 17.4 %copy-start.13 = (f32[512,128]{1,0:T(8,128)S(1)}, f32[512,128]{1,0:T(8,128)}, u32[]{:S(2)}) copy-start(f32[512,128]{1,0:T(8,128)} %copy-done.11) | copy-start | bytes 786436
  117.9 17.4 %copy-start.24 = (f32[512,128]{1,0:T(8,128)S(1)}, f32[512,128]{1,0:T(8,128)}, u32[]{:S(2)}) copy-start(f32[512,128]{1,0:T(8,128)} %copy-done.23) | copy-start | bytes 786436
  158.6 18.7 %copy-start.22 = (f32[8,8,192]{2,1,0:T(8,128)S(1)}, f32[8,8,192]{2,1,0:T(8,128)}, u32[]{:S(2)}) copy-start(f32[8,8,192]{2,1,0:T(8,128)} %copy-done.20) | copy-start | bytes 147460
  158.6 18.7 %copy-start.26 = (f32[8,8,192]{2,1,0:T(8,128)S(1)}, f32[8,8,192]{2,1,0:T(8,128)}, u32[]{:S(2)}) copy-start(f32[8,8,192]{2,1,0:T(8,128)} %copy-done.25) | copy-start | bytes 147460
  159.4 17.9 %all-to-all-start.6 = ((f32[8,8,128]{2,1,0:T(8,128)}), f32[8,8,128]{2,1,0:T(8,128)S(1)}, u32[]{:S(2)}, u32[]{:S(2)}) async-start(f32[8,8,128]{2,1,0:T(8,128)} %bitcast.3), calls=%async_computation.6 | async-start | bytes 65536 | tf_op jit(solution)/shard_map/all_to_all | solution.py:308

commit v2 on v1

--- a/solution.py
+++ b/solution.py
@@ -25,7 +25,7 @@
 MSG = KB + 1
 TB = SAMPLES // AF
 LAST = 3 * TB + 1
-VMEM = 48 * 1024 * 1024
+VMEM = 16 * 1024 * 1024
 
 
 def dft_tables():
@@ -261,7 +261,8 @@
 
 
 def exchange(message):
-    return lax.all_to_all(message, "af", split_axis=0, concat_axis=0, tiled=True)
+    flat = message.reshape(AF, 1, message.shape[0] // AF * 128)
+    return lax.all_to_all(flat, "af", split_axis=0, concat_axis=0, tiled=True).reshape(message.shape)
 
 
 def per_device(recorded, kernel, cutoff):

time: 180 us -> 143 us (0.79)
  local copies, waits for them, and re-layouts: 27.8 us -> 7.63 us
  blocking collectives: 92.5 us -> 81.6 us
  Pallas kernels: 15.6 us -> 13.7 us
  waiting for transfers between devices: 16.3 us -> 14.4 us
    all_to_all x12 -> x0, local copies, waits for them, and re-layouts: 11.3 us -> none  [exchange(): lax.all_to_all(message, 'af', split_axis=0, concat_axis=0, tiled=True)]
    all_to_all x5, blocking collectives: 92.5 us -> 81.6 us  [exchange(): lax.all_to_all(flat, 'af', split_axis=0, concat_axis=0, tiled=True)]
    unnamed x54 -> x24, local copies, waits for them, and re-layouts: 16.5 us -> 7.62 us
    pallas_call x8, Pallas kernels: 15.6 us -> 13.7 us  [call(): pl.pallas_call(body, out_shape=[jax.ShapeDtypeStruct(s, t) for s, t in ou...]
    all_to_all x1, waiting for transfers between devices: 11.6 us -> 9.73 us  [exchange(): lax.all_to_all(flat, 'af', split_axis=0, concat_axis=0, tiled=True)]
where the time goes in v2:
time: 143 us
  blocking collectives  81.6 us (57%)
  starting transfers between devices  24.4 us (17%)
  waiting for transfers between devices  14.4 us (10%)
  Pallas kernels  13.7 us (10%)
  local copies, waits for them, and re-layouts  7.63 us (5%)
    all_to_all x5, blocking collectives, exchange(): lax.all_to_all(flat, 'af', split_axis=0, concat_axis=0, tiled=True)  81.6 us
    pallas_call x8, Pallas kernels, call(): pl.pallas_call(body, out_shape=[jax.ShapeDtypeStruct(s, t) for s, t in ou...  13.7 us
    all_to_all x1, starting transfers between devices, per_device(): lax.all_to_all(stats, 'vert', split_axis=0, concat_axis=0, tiled=True)  12.3 us
    all_to_all x1, starting transfers between devices, exchange(): lax.all_to_all(flat, 'af', split_axis=0, concat_axis=0, tiled=True)  12.2 us
    all_to_all x1, waiting for transfers between devices, exchange(): lax.all_to_all(flat, 'af', split_axis=0, concat_axis=0, tiled=True)  9.73 us
    unnamed x24, local copies, waits for them, and re-layouts  7.62 us
    all_to_all x1, waiting for transfers between devices, per_device(): lax.all_to_all(stats, 'vert', split_axis=0, concat_axis=0, tiled=True)  4.72 us
  transfers between devices with their start and end apart: 2, of which 2 were waited for; matrix products, arithmetic and copies ran while one was open for 0% of the time, Pallas kernels for 0%

profile of v2, /device:TPU:1, one launch (start us, length us, event | category | flops | bytes accessed | tf_op | source)
XLA Modules:
  0.0 142.6 jit_solution(16015143924968282713)
XLA Ops:
  0.6 0.0 copy-start
  0.6 0.0 copy-start.4
  0.7 1.9 %copy-done.4 = f32[8,2,96,512]{3,2,1,0:T(8,128)S(1)} copy-done((f32[8,2,96,512]{3,2,1,0:T(8,128)S(1)}, f32[8,2,96,512]{3,2,1,0:T(8,128)}, u32[]{:S(2)}) %copy-start.4) | copy-done | bytes 3145752
  2.5 0.0 copy-start.9
  2.5 0.8 copy-done.9
  3.4 0.9 shard_map.94
  4.3 0.7 copy-done.11
  5.0 12.2 %all-to-all-start = ((f32[32,1,2176]{2,1,0:T(1,128)}), f32[32,1,2176]{2,1,0:T(1,128)S(1)}, u32[]{:S(2)}, u32[]{:S(2)}) async-start(f32[32,1,2176]{2,1,0:T(1,128)} %bitcast.27), calls=%async_computation | async-start | bytes 557056 | tf_op jit(solution)/shard_map/all_to_all | solution.py:265
  17.2 0.0 copy-done
  17.2 9.7 %all-to-all-done = f32[32,1,2176]{2,1,0:T(1,128)S(1)} async-done(((f32[32,1,2176]{2,1,0:T(1,128)}), f32[32,1,2176]{2,1,0:T(1,128)S(1)}, u32[]{:S(2)}, u32[]{:S(2)}) %all-to-all-start) | async-done | bytes 278560 | tf_op jit(solution)/shard_map/all_to_all | solution.py:265
  27.0 1.0 copy-done.1
  28.0 1.0 copy-done.3
  29.1 1.0 copy-done.5
  30.1 1.0 copy-done.7
  31.1 0.8 shard_map.95
  31.9 16.0 %all_to_all.41 = f32[32,1,2176]{2,1,0:T(1,128)S(1)} all-to-all(f32[32,1,2176]{2,1,0:T(1,128)S(1)} %bitcast.31), channel_id=1, replica_groups=mesh['af'=32,'vert'=8] {'af'}, dimensions={0} | all-to-all | bytes 557056 | tf_op jit(solution)/shard_map/all_to_all | solution.py:265
  47.9 0.0 copy-done.10
  47.9 4.5 %shard_map.96 = (f32[544,128]{1,0:T(8,128)S(1)}, f32[8,8,192]{2,1,0:T(8,128)S(1)}, f32[8,128]{1,0:T(8,128)S(1)}) custom-call(f32[544,128]{1,0:T(8,128)S(1)} %bitcast.25, bf16[8,192,512]{2,1,0:T(8,128)(2,1)S(1)} %get-tuple-element.22.khi_ref, bf16[8,192,512]{2,1,0:T(8,128)(2,1)S(1)} %get-tuple-element.23.klo_ref, f32[8,8,192]{2,1,0:T(8,128)S(1)} %copy-done.10, ...), custom_call_target="tpu_custom_call" | custom-call | tf_op jit(solution)/shard_map/pallas_call | solution.py:253
  52.4 15.7 %all_to_all.42 = f32[32,1,2176]{2,1,0:T(1,128)S(1)} all-to-all(f32[32,1,2176]{2,1,0:T(1,128)S(1)} %bitcast.30), channel_id=1, replica_groups=mesh['af'=32,'vert'=8] {'af'}, dimensions={0} | all-to-all | bytes 557056 | tf_op jit(solution)/shard_map/all_to_all | solution.py:265
  68.1 0.0 copy-done.2
  68.1 0.0 copy-done.6
  68.1 0.0 copy-done.8
  68.1 0.8 shard_map.97
  68.9 14.8 %all_to_all.43 = f32[32,1,2176]{2,1,0:T(1,128)S(1)} all-to-all(f32[32,1,2176]{2,1,0:T(1,128)S(1)} %bitcast.28), channel_id=1, replica_groups=mesh['af'=32,'vert'=8] {'af'}, dimensions={0} | all-to-all | bytes 557056 | tf_op jit(solution)/shard_map/all_to_all | solution.py:265
  83.7 4.5 %shard_map.98 = (f32[544,128]{1,0:T(8,128)S(1)}, f32[8,8,192]{2,1,0:T(8,128)S(1)}, f32[8,128]{1,0:T(8,128)S(1)}) custom-call(f32[544,128]{1,0:T(8,128)S(1)} %bitcast.24, bf16[8,192,512]{2,1,0:T(8,128)(2,1)S(1)} %get-tuple-element.22.khi_ref, bf16[8,192,512]{2,1,0:T(8,128)(2,1)S(1)} %get-tuple-element.23.klo_ref, ...), custom_call_target="tpu_custom_call" | custom-call | tf_op jit(solution)/shard_map/pallas_call | solution.py:253
  88.2 14.2 %all_to_all.44 = f32[32,1,2176]{2,1,0:T(1,128)S(1)} all-to-all(f32[32,1,2176]{2,1,0:T(1,128)S(1)} %bitcast.29), channel_id=1, replica_groups=mesh['af'=32,'vert'=8] {'af'}, dimensions={0} | all-to-all | bytes 557056 | tf_op jit(solution)/shard_map/all_to_all | solution.py:265
  102.4 0.5 shard_map.99
  102.9 21.0 %all_to_all.45 = f32[32,1,6272]{2,1,0:T(1,128)S(1)} all-to-all(f32[32,1,6272]{2,1,0:T(1,128)S(1)} %bitcast.26), channel_id=1, replica_groups=mesh['af'=32,'vert'=8] {'af'}, dimensions={0} | all-to-all | bytes 1605632 | tf_op jit(solution)/shard_map/all_to_all | solution.py:265
  123.8 0.7 shard_map.100
  124.6 12.3 %all-to-all-start.6 = ((f32[8,8,128]{2,1,0:T(8,128)}), f32[8,8,128]{2,1,0:T(8,128)S(1)}, u32[]{:S(2)}, u32[]{:S(2)}) async-start(f32[8,8,128]{2,1,0:T(8,128)} %bitcast.15), calls=%async_computation.6 | async-start | bytes 65536 | tf_op jit(solution)/shard_map/all_to_all | solution.py:309
  136.8 4.7 %all-to-all-done.6 = f32[8,8,128]{2,1,0:T(8,128)S(1)} async-done(((f32[8,8,128]{2,1,0:T(8,128)}), f32[8,8,128]{2,1,0:T(8,128)S(1)}, u32[]{:S(2)}, u32[]{:S(2)}) %all-to-all-start.6) | async-done | bytes 32800 | tf_op jit(solution)/shard_map/all_to_all | solution.py:309
  141.5 1.1 shard_map.101
  (10 shorter events, 0.0 us)
Async XLA Ops:
  0.6 16.6 %copy-start = (s32[512]{0:T(512)S(1)}, s32[512]{0:T(512)}, u32[]{:S(2)}) copy-start(s32[512]{0:T(512)} %param.9) | copy-start | bytes 6148
  0.6 1.9 %copy-start.4 = (f32[8,2,96,512]{3,2,1,0:T(8,128)S(1)}, f32[8,2,96,512]{3,2,1,0:T(8,128)}, u32[]{:S(2)}) copy-start(f32[8,2,96,512]{3,2,1,0:T(8,128)} %param.8) | copy-start | bytes 9437188
  2.5 0.8 copy-start.9
  4.3 0.7 copy-start.11
  5.0 42.9 %copy-start.10 = (f32[8,8,192]{2,1,0:T(8,128)S(1)}, f32[8,8,192]{2,1,0:T(8,128)}, u32[]{:S(2)}) copy-start(f32[8,8,192]{2,1,0:T(8,128)} %q0_ref.1) | copy-start | bytes 147460
  5.0 21.9 %all-to-all-start = ((f32[32,1,2176]{2,1,0:T(1,128)}), f32[32,1,2176]{2,1,0:T(1,128)S(1)}, u32[]{:S(2)}, u32[]{:S(2)}) async-start(f32[32,1,2176]{2,1,0:T(1,128)} %bitcast.27), calls=%async_computation | async-start | bytes 557056 | tf_op jit(solution)/shard_map/all_to_all | solution.py:265
  27.0 1.0 copy-start.1
  28.0 1.0 copy-start.3
  29.0 1.0 copy-start.5
  30.1 1.0 copy-start.7
  47.9 20.2 %copy-start.2 = (bf16[512,512]{1,0:T(8,128)(2,1)S(1)}, bf16[512,512]{1,0:T(8,128)(2,1)}, u32[]{:S(2)}) copy-start(bf16[512,512]{1,0:T(8,128)(2,1)} %constant.32.clone.refs_3_) | copy-start | bytes 1572868
  47.9 20.2 %copy-start.6 = (bf16[512,512]{1,0:T(8,128)(2,1)S(1)}, bf16[512,512]{1,0:T(8,128)(2,1)}, u32[]{:S(2)}) copy-start(bf16[512,512]{1,0:T(8,128)(2,1)} %constant.34.clone.refs_5_) | copy-start | bytes 1572868
  47.9 20.2 %copy-start.8 = (bf16[512,512]{1,0:T(8,128)(2,1)S(1)}, bf16[512,512]{1,0:T(8,128)(2,1)}, u32[]{:S(2)}) copy-start(bf16[512,512]{1,0:T(8,128)(2,1)} %constant.33.clone.refs_4_) | copy-start | bytes 1572868
  124.6 17.0 %all-to-all-start.6 = ((f32[8,8,128]{2,1,0:T(8,128)}), f32[8,8,128]{2,1,0:T(8,128)S(1)}, u32[]{:S(2)}, u32[]{:S(2)}) async-start(f32[8,8,128]{2,1,0:T(8,128)} %bitcast.15), calls=%async_computation.6 | async-start | bytes 65536 | tf_op jit(solution)/shard_map/all_to_all | solution.py:309

commit v3 on v2

--- a/solution.py
+++ b/solution.py
@@ -1,3 +1,4 @@
+import functools
 import math
 
 import jax
@@ -25,7 +26,6 @@
 MSG = KB + 1
 TB = SAMPLES // AF
 LAST = 3 * TB + 1
-VMEM = 16 * 1024 * 1024
 
 
 def dft_tables():
@@ -39,7 +39,7 @@
     for t in (table, np.ascontiguousarray(table.T)):
         hi = t.astype(jnp.bfloat16)
         out += [hi, (t - hi.astype(np.float32)).astype(jnp.bfloat16)]
-    return out
+    return np.stack(out)
 
 
 def split(x):
@@ -99,16 +99,26 @@
         msg[pl.ds(d * pitch + pitch - 1, 1), :] = row
 
 
-def first_kernel(u_ref, k_ref, msg, khi_ref, klo_ref):
+def first_kernel(u_hbm, k_hbm, t_hbm, msg, khi_ref, klo_ref, t_ref, u_buf, k_buf, sems):
+    u_copy = pltpu.make_async_copy(u_hbm, u_buf, sems.at[FB])
+    k_copies = [pltpu.make_async_copy(k_hbm.at[f], k_buf.at[f], sems.at[f]) for f in range(FB)]
+    t_copy = pltpu.make_async_copy(t_hbm, t_ref, sems.at[FB + 1])
+    u_copy.start()
+    for copy in k_copies:
+        copy.start()
+    t_copy.start()
+    u_copy.wait()
     square = jnp.zeros((VB, 2 * SRCS), F32)
     for f in range(FB):
-        u = u_ref[f]
+        u = u_buf[f]
         square += u * u
-        khi, klo = split(k_ref[f])
+        k_copies[f].wait()
+        khi, klo = split(k_buf[f])
         khi_ref[f] = khi
         klo_ref[f] = klo
         put_spectra(msg, f, kernel_adjoint(u, khi, klo))
     put_partial(msg, lane_zero(jnp.sum(square, keepdims=True)), MSG)
+    t_copy.wait()
 
 
 def data_kernel(order, recv, khi_ref, klo_ref, before_ref, stats, msg, q_ref, stats_out):
@@ -117,8 +127,8 @@
     stats_out[pl.ds(order, 1), :] = total
     coefficient = ratio(total, stats[pl.ds(order - 1, 1), :])[:, :1]
     square = jnp.zeros((VB, 2 * SRCS), F32)
+    steps = []
     for f in range(FB):
-        khi, klo = khi_ref[f], klo_ref[f]
         x = jnp.concatenate(
             [
                 jnp.concatenate(
@@ -132,35 +142,35 @@
             ],
             axis=0,
         )
-        u = kernel_forward(x, khi, klo) - coefficient * before_ref[f]
+        u = kernel_forward(x, khi_ref[f], klo_ref[f]) - coefficient * before_ref[f]
         q_ref[f] = u
         square += u * u
-        put_spectra(msg, f, kernel_adjoint(u, khi, klo))
+        steps.append(u)
+    for f in range(FB):
+        put_spectra(msg, f, kernel_adjoint(steps[f], khi_ref[f], klo_ref[f]))
     put_partial(msg, lane_zero(jnp.sum(square, keepdims=True)), MSG)
 
 
-def table_apply(hi_ref, lo_ref, x):
+def table_apply(table_ref, at, x):
     hi, lo = split(x)
-    both = dot(hi_ref[...], jnp.concatenate([hi, lo], axis=1))
-    return both[:, :128] + both[:, 128:] + dot(lo_ref[...], hi)
+    both = dot(table_ref[at], jnp.concatenate([hi, lo], axis=1))
+    return both[:, :128] + both[:, 128:] + dot(table_ref[at + 1], hi)
 
 
 def model_kernel(order, last, *refs):
     refs = list(refs)
-    recv, cut_ref, inv_hi, inv_lo = refs[:4]
-    refs = refs[4:]
-    if not last:
-        fwd_hi, fwd_lo = refs[:2]
-        refs = refs[2:]
+    recv, cut_ref, table_ref = refs[:3]
+    refs = refs[3:]
     if order > 0:
         stats = refs.pop(0)
         earlier = [refs.pop(0) for _ in range(order // 2)]
     total = arrived_sum(recv, MSG)
     spectra = jnp.concatenate([recv[pl.ds(p * MSG, KB), :] for p in range(AF)], axis=0)
-    s = table_apply(inv_hi, inv_lo, spectra)
+    s = table_apply(table_ref, 0, spectra)
     if order > 0:
         s = s - ratio(total, stats[pl.ds(order - 1, 1), :]) * earlier[-1][...]
-    keep = lax.broadcasted_iota(jnp.int32, (SAMPLES, 128), 0) < cut_ref[...]
+    cut = cut_ref[pl.ds(lax.rem(lax.axis_index("af"), QB), 1), :]
+    keep = lax.broadcasted_iota(jnp.int32, (SAMPLES, 128), 0) < cut
     s = jnp.where(keep, s, 0.0)
     partial = jnp.sum(s * s, axis=0, keepdims=True)
     if last:
@@ -176,7 +186,7 @@
                 msg[pl.ds(p * LAST + j * TB, TB), :] = value[p * TB : (p + 1) * TB]
         put_partial(msg, partial, LAST)
     else:
-        out = table_apply(fwd_hi, fwd_lo, s)
+        out = table_apply(table_ref, 2, s)
         for p in range(AF):
             msg[pl.ds(p * MSG, KB), :] = out[p * KB : (p + 1) * KB]
         put_partial(msg, partial, MSG)
@@ -190,7 +200,7 @@
         out[pl.ds(8 * g, 8), :] = mine
 
 
-def last_kernel(group_ref, recv, gathered, q0_ref, q1_ref, q2_ref, sol_ref, dir_ref, left_ref, rows):
+def last_kernel(recv, gathered, q0_ref, q1_ref, q2_ref, sol_ref, dir_ref, left_ref, rows):
     n0, m1, n1, m2, n2, m3 = [gathered[pl.ds(j, VERT, stride=8), :] for j in range(6)]
 
     def norm(x):
@@ -235,7 +245,7 @@
     y3 = z3 / alpha3
     for j, value in enumerate((x1, x2, y1, y2, y3, c0, c1, c2)):
         rows[pl.ds(8 * j, 8), :] = jnp.broadcast_to(value, (VERT, 128))
-    group = group_ref[0]
+    group = lax.axis_index("vert")
     x1, x2, y1, y2, y3, c0, c1, c2 = [rows[pl.ds(8 * j + group, 1), :] for j in range(8)]
     for v in range(VB):
         for q in range(QB):
@@ -248,29 +258,27 @@
         left_ref[f] = c0 * q0_ref[f] + c1 * q1_ref[f] + c2 * q2_ref[f]
 
 
-def call(body, outs, *operands, scratch=(), smem=0):
-    vmem = pl.BlockSpec(memory_space=pltpu.VMEM)
+def call(body, outs, *operands, scratch=(), space=pltpu.VMEM, vmem=16):
+    here = pl.BlockSpec(memory_space=pltpu.VMEM)
     return pl.pallas_call(
         body,
         out_shape=[jax.ShapeDtypeStruct(s, t) for s, t in outs],
-        in_specs=[pl.BlockSpec(memory_space=pltpu.SMEM)] * smem + [vmem] * (len(operands) - smem),
-        out_specs=[vmem] * len(outs),
+        in_specs=[pl.BlockSpec(memory_space=space)] * len(operands),
+        out_specs=[here] * len(outs),
         scratch_shapes=list(scratch),
-        compiler_params=pltpu.CompilerParams(vmem_limit_bytes=VMEM),
+        compiler_params=pltpu.CompilerParams(vmem_limit_bytes=vmem * 1024 * 1024),
     )(*operands)
 
 
 def exchange(message):
     flat = message.reshape(AF, 1, message.shape[0] // AF * 128)
-    return lax.all_to_all(flat, "af", split_axis=0, concat_axis=0, tiled=True).reshape(message.shape)
+    flat = lax.all_to_all(flat, "af", split_axis=0, concat_axis=0, tiled=True)
+    return flat.reshape(message.shape)
 
 
 def per_device(recorded, kernel, cutoff):
-    import functools
-
-    inv_hi, inv_lo, fwd_hi, fwd_lo = [jnp.asarray(t) for t in dft_tables()]
-    place = lax.axis_index("af")
-    cut = lax.dynamic_slice(cutoff.reshape(QB, 128), (place % QB, 0), (1, 128))
+    tables = jnp.asarray(dft_tables())
+    cut = cutoff.reshape(QB, 128)
     kernel = kernel.reshape(FB, 2 * SRCS, RECV)
     message = ((AF * MSG, 128), F32)
     data = ((FB, VB, 2 * SRCS), F32)
@@ -278,11 +286,22 @@
     stat = ((8, 128), F32)
     wide = ((FB, 2 * SRCS, RECV), BF16)
 
-    msg, khi, klo = call(first_kernel, [message, wide, wide], recorded, kernel)
+    msg, khi, klo, tables = call(
+        first_kernel,
+        [message, wide, wide, (tables.shape, BF16)],
+        recorded, kernel, tables,
+        scratch=[
+            pltpu.VMEM(recorded.shape, F32),
+            pltpu.VMEM(kernel.shape, F32),
+            pltpu.SemaphoreType.DMA((FB + 2,)),
+        ],
+        space=pltpu.HBM,
+        vmem=47,
+    )
     msg, s1, stats = call(
         functools.partial(model_kernel, 0, False),
         [message, model, stat],
-        exchange(msg), cut, inv_hi, inv_lo, fwd_hi, fwd_lo,
+        exchange(msg), cut, tables,
     )
     msg, q1, stats = call(
         functools.partial(data_kernel, 1),
@@ -292,7 +311,7 @@
     msg, s2, stats = call(
         functools.partial(model_kernel, 2, False),
         [message, model, stat],
-        exchange(msg), cut, inv_hi, inv_lo, fwd_hi, fwd_lo, stats, s1,
+        exchange(msg), cut, tables, stats, s1,
     )
     msg, q2, stats = call(
         functools.partial(data_kernel, 3),
@@ -302,20 +321,18 @@
     msg, stats = call(
         functools.partial(model_kernel, 4, True),
         [((AF * LAST, 128), F32), stat],
-        exchange(msg), cut, inv_hi, inv_lo, stats, s1, s2,
+        exchange(msg), cut, tables, stats, s1, s2,
     )
     arrived = exchange(msg)
     [stats] = call(stats_kernel, [((VERT * 8, 128), F32)], arrived, stats)
     gathered = lax.all_to_all(stats, "vert", split_axis=0, concat_axis=0, tiled=True)
-    group = lax.axis_index("vert").astype(jnp.int32).reshape(1)
     out = ((VB, TB, RECV), F32)
     return tuple(
         call(
             last_kernel,
             [out, out, data],
-            group, arrived, gathered, recorded, q1, q2,
+            arrived, gathered, recorded, q1, q2,
             scratch=[pltpu.VMEM((64, 128), F32)],
-            smem=1,
         )
     )
 

time: 143 us -> 131 us (0.916)
  blocking collectives: 81.6 us -> 120 us
  starting transfers between devices: 24.4 us -> 0 us
  waiting for transfers between devices: 14.4 us -> 0 us
  local copies, waits for them, and re-layouts: 7.63 us -> 0.84 us
  Pallas kernels: 13.7 us -> 9.1 us
    all_to_all x5 -> x7, blocking collectives: 81.6 us -> 120 us  [the longest x6 103 us: exchange(): flat = lax.all_to_all(flat, 'af', split_axis=0, concat_axis=0, tiled=True)]
    all_to_all x2 -> x0, starting transfers between devices: 24.4 us -> none  [the longest x1 12.3 us: per_device(): lax.all_to_all(stats, 'vert', split_axis=0, concat_axis=0, tiled=True)]
    all_to_all x2 -> x0, waiting for transfers between devices: 14.4 us -> none  [the longest x1 9.73 us: exchange(): lax.all_to_all(flat, 'af', split_axis=0, concat_axis=0, tiled=True)]
    unnamed x24 -> x4, local copies, waits for them, and re-layouts: 7.62 us -> 0.84 us
    pallas_call x8, Pallas kernels: 13.7 us -> 9.1 us  [call(): pl.pallas_call(body, out_shape=[jax.ShapeDtypeStruct(s, t) for s, t in ou...]
  transfers between devices with their start and end apart: 2 -> 0, of which waited for: 2 -> 0; matrix products, arithmetic and copies ran while one was open for 0% -> 0% of each run, Pallas kernels for 0% -> 0%
where the time goes in v3:
time: 131 us
  blocking collectives  120 us (92%)
  Pallas kernels  9.1 us (7%)
    all_to_all x6, blocking collectives, exchange(): flat = lax.all_to_all(flat, 'af', split_axis=0, concat_axis=0, tiled=True)  103 us
    all_to_all x1, blocking collectives, per_device(): lax.all_to_all(stats, 'vert', split_axis=0, concat_axis=0, tiled=True)  16.8 us
    pallas_call x8, Pallas kernels, call(): pl.pallas_call(body, out_shape=[jax.ShapeDtypeStruct(s, t) for s, t in ou...  9.1 us

profile of v3, /device:TPU:1, one launch (start us, length us, event | category | flops | bytes accessed | tf_op | source)
XLA Modules:
  0.0 130.6 jit_solution(3940773397889756288)
XLA Ops:
  0.6 0.0 copy-start
  0.6 0.8 copy-done
  1.5 0.0 copy-start.1
  1.5 2.9 %shard_map.67 = (f32[544,128]{1,0:T(8,128)S(1)}, bf16[8,192,512]{2,1,0:T(8,128)(2,1)S(1)}, bf16[8,192,512]{2,1,0:T(8,128)(2,1)S(1)}, bf16[4,512,512]{2,1,0:T(8,128)(2,1)S(1)}) custom-call(f32[8,8,192]{2,1,0:T(8,128)S(1)} %copy-done, f32[8,192,512]{2,1,0:T(8,128)} %bitcast.34, bf16[4,512,512]{2,1,0:T(8,128)(2,1)} %constant.2.clone.t_hbm), custom_call_target="tpu_custom_call" | custom-call | tf_op jit(solution)/shard_map/pallas_call | solution.py:263
  4.4 21.6 %all_to_all.41 = f32[32,1,2176]{2,1,0:T(1,128)S(1)} all-to-all(f32[32,1,2176]{2,1,0:T(1,128)S(1)} %bitcast.25), channel_id=1, replica_groups=mesh['af'=32,'vert'=8] {'af'}, dimensions={0} | all-to-all | bytes 557056 | tf_op jit(solution)/shard_map/all_to_all | solution.py:275
  26.0 0.0 copy-done.1
  26.0 0.8 shard_map.68
  26.8 16.0 %all_to_all.42 = f32[32,1,2176]{2,1,0:T(1,128)S(1)} all-to-all(f32[32,1,2176]{2,1,0:T(1,128)S(1)} %bitcast.28), channel_id=1, replica_groups=mesh['af'=32,'vert'=8] {'af'}, dimensions={0} | all-to-all | bytes 557056 | tf_op jit(solution)/shard_map/all_to_all | solution.py:275
  42.8 1.5 %shard_map.69 = (f32[544,128]{1,0:T(8,128)S(1)}, f32[8,8,192]{2,1,0:T(8,128)S(1)}, f32[8,128]{1,0:T(8,128)S(1)}) custom-call(f32[544,128]{1,0:T(8,128)S(1)} %bitcast.21, bf16[8,192,512]{2,1,0:T(8,128)(2,1)S(1)} %get-tuple-element.24.khi_ref, bf16[8,192,512]{2,1,0:T(8,128)(2,1)S(1)} %get-tuple-element.25.klo_ref, f32[8,8,192]{2,1,0:T(8,128)S(1)} %copy-done, ...), custom_call_target="tpu_custom_call" | custom-call | tf_op jit(solution)/shard_map/pallas_call | solution.py:263
  44.2 15.7 %all_to_all.43 = f32[32,1,2176]{2,1,0:T(1,128)S(1)} all-to-all(f32[32,1,2176]{2,1,0:T(1,128)S(1)} %bitcast.26), channel_id=1, replica_groups=mesh['af'=32,'vert'=8] {'af'}, dimensions={0} | all-to-all | bytes 557056 | tf_op jit(solution)/shard_map/all_to_all | solution.py:275
  59.9 0.8 shard_map.70
  60.7 14.9 %all_to_all.44 = f32[32,1,2176]{2,1,0:T(1,128)S(1)} all-to-all(f32[32,1,2176]{2,1,0:T(1,128)S(1)} %bitcast.27), channel_id=1, replica_groups=mesh['af'=32,'vert'=8] {'af'}, dimensions={0} | all-to-all | bytes 557056 | tf_op jit(solution)/shard_map/all_to_all | solution.py:275
  75.6 1.5 %shard_map.71 = (f32[544,128]{1,0:T(8,128)S(1)}, f32[8,8,192]{2,1,0:T(8,128)S(1)}, f32[8,128]{1,0:T(8,128)S(1)}) custom-call(f32[544,128]{1,0:T(8,128)S(1)} %bitcast.20, bf16[8,192,512]{2,1,0:T(8,128)(2,1)S(1)} %get-tuple-element.24.khi_ref, bf16[8,192,512]{2,1,0:T(8,128)(2,1)S(1)} %get-tuple-element.25.klo_ref, ...), custom_call_target="tpu_custom_call" | custom-call | tf_op jit(solution)/shard_map/pallas_call | solution.py:263
  77.1 14.2 %all_to_all.45 = f32[32,1,2176]{2,1,0:T(1,128)S(1)} all-to-all(f32[32,1,2176]{2,1,0:T(1,128)S(1)} %bitcast.24), channel_id=1, replica_groups=mesh['af'=32,'vert'=8] {'af'}, dimensions={0} | all-to-all | bytes 557056 | tf_op jit(solution)/shard_map/all_to_all | solution.py:275
  91.2 0.5 shard_map.72
  91.7 21.0 %all_to_all.46 = f32[32,1,6272]{2,1,0:T(1,128)S(1)} all-to-all(f32[32,1,6272]{2,1,0:T(1,128)S(1)} %bitcast.23), channel_id=1, replica_groups=mesh['af'=32,'vert'=8] {'af'}, dimensions={0} | all-to-all | bytes 1605632 | tf_op jit(solution)/shard_map/all_to_all | solution.py:275
  112.7 0.1 shard_map.73
  112.8 16.8 %all_to_all.47 = f32[8,8,128]{2,1,0:T(8,128)S(1)} all-to-all(f32[8,8,128]{2,1,0:T(8,128)S(1)} %bitcast.30), channel_id=1, replica_groups=mesh['af'=32,'vert'=8] {'vert'}, dimensions={0} | all-to-all | bytes 65536 | tf_op jit(solution)/shard_map/all_to_all | solution.py:328
  129.6 1.1 shard_map.74
Async XLA Ops:
  0.6 0.8 copy-start
  1.5 24.5 %copy-start.1 = (s32[512]{0:T(512)S(1)}, s32[512]{0:T(512)}, u32[]{:S(2)}) copy-start(s32[512]{0:T(512)} %param.6) | copy-start | bytes 6148

commit v4 on v3

--- a/solution.py
+++ b/solution.py
@@ -26,6 +26,7 @@
 MSG = KB + 1
 TB = SAMPLES // AF
 LAST = 3 * TB + 1
+CHUNKS = ((0, 2), (2, 2), (4, 2), (6, 2))
 
 
 def dft_tables():
@@ -99,26 +100,26 @@
         msg[pl.ds(d * pitch + pitch - 1, 1), :] = row
 
 
-def first_kernel(u_hbm, k_hbm, t_hbm, msg, khi_ref, klo_ref, t_ref, u_buf, k_buf, sems):
-    u_copy = pltpu.make_async_copy(u_hbm, u_buf, sems.at[FB])
-    k_copies = [pltpu.make_async_copy(k_hbm.at[f], k_buf.at[f], sems.at[f]) for f in range(FB)]
-    t_copy = pltpu.make_async_copy(t_hbm, t_ref, sems.at[FB + 1])
-    u_copy.start()
-    for copy in k_copies:
+def halves_kernel(k_hbm, khi_ref, klo_ref, k_buf, sems):
+    copies = [
+        pltpu.make_async_copy(k_hbm.at[pl.ds(at, n)], k_buf.at[pl.ds(at, n)], sems.at[i])
+        for i, (at, n) in enumerate(CHUNKS)
+    ]
+    for copy in copies:
         copy.start()
-    t_copy.start()
-    u_copy.wait()
+    for copy, (at, n) in zip(copies, CHUNKS):
+        copy.wait()
+        for f in range(at, at + n):
+            khi_ref[f], klo_ref[f] = split(k_buf[f])
+
+
+def first_kernel(u_ref, khi_ref, klo_ref, msg):
     square = jnp.zeros((VB, 2 * SRCS), F32)
     for f in range(FB):
-        u = u_buf[f]
+        u = u_ref[f]
         square += u * u
-        k_copies[f].wait()
-        khi, klo = split(k_buf[f])
-        khi_ref[f] = khi
-        klo_ref[f] = klo
-        put_spectra(msg, f, kernel_adjoint(u, khi, klo))
+        put_spectra(msg, f, kernel_adjoint(u, khi_ref[f], klo_ref[f]))
     put_partial(msg, lane_zero(jnp.sum(square, keepdims=True)), MSG)
-    t_copy.wait()
 
 
 def data_kernel(order, recv, khi_ref, klo_ref, before_ref, stats, msg, q_ref, stats_out):
@@ -286,18 +287,15 @@
     stat = ((8, 128), F32)
     wide = ((FB, 2 * SRCS, RECV), BF16)
 
-    msg, khi, klo, tables = call(
-        first_kernel,
-        [message, wide, wide, (tables.shape, BF16)],
-        recorded, kernel, tables,
-        scratch=[
-            pltpu.VMEM(recorded.shape, F32),
-            pltpu.VMEM(kernel.shape, F32),
-            pltpu.SemaphoreType.DMA((FB + 2,)),
-        ],
+    khi, klo = call(
+        halves_kernel,
+        [wide, wide],
+        kernel,
+        scratch=[pltpu.VMEM(kernel.shape, F32), pltpu.SemaphoreType.DMA((len(CHUNKS),))],
         space=pltpu.HBM,
-        vmem=47,
-    )
+        vmem=49,
+    )
+    [msg] = call(first_kernel, [message], recorded, khi, klo)
     msg, s1, stats = call(
         functools.partial(model_kernel, 0, False),
         [message, model, stat],

time: 131 us -> 130 us (level)
    pallas_call x8 -> x9, Pallas kernels: 9.1 us -> 8.88 us  [call(): pl.pallas_call(body, out_shape=[jax.ShapeDtypeStruct(s, t) for s, t in ou...]
where the time goes in v4:
time: 130 us
  blocking collectives  120 us (92%)
  Pallas kernels  8.88 us (7%)
    all_to_all x6, blocking collectives, exchange(): flat = lax.all_to_all(flat, 'af', split_axis=0, concat_axis=0, tiled=True)  103 us
    all_to_all x1, blocking collectives, per_device(): lax.all_to_all(stats, 'vert', split_axis=0, concat_axis=0, tiled=True)  16.8 us
    pallas_call x9, Pallas kernels, call(): pl.pallas_call(body, out_shape=[jax.ShapeDtypeStruct(s, t) for s, t in ou...  8.88 us

profile of v4, /device:TPU:1, one launch (start us, length us, event | category | flops | bytes accessed | tf_op | source)
XLA Modules:
  0.0 129.6 jit_solution(10383832316598668805)
XLA Ops:
  0.6 0.0 copy-start.1
  0.6 2.0 %shard_map.67 = (bf16[8,192,512]{2,1,0:T(8,128)(2,1)S(1)}, bf16[8,192,512]{2,1,0:T(8,128)(2,1)S(1)}) custom-call(f32[8,192,512]{2,1,0:T(8,128)} %bitcast.34), custom_call_target="tpu_custom_call" | custom-call | tf_op jit(solution)/shard_map/pallas_call | solution.py:264
  2.7 0.0 copy-start
  2.7 0.0 copy-start.2
  2.7 0.0 copy-done.1
  2.7 0.6 shard_map.68
  3.4 21.6 %all_to_all.41 = f32[32,1,2176]{2,1,0:T(1,128)S(1)} all-to-all(f32[32,1,2176]{2,1,0:T(1,128)S(1)} %bitcast.23), channel_id=1, replica_groups=mesh['af'=32,'vert'=8] {'af'}, dimensions={0} | all-to-all | bytes 557056 | tf_op jit(solution)/shard_map/all_to_all | solution.py:276
  25.0 0.0 copy-done
  25.0 0.0 copy-done.2
  25.0 0.8 shard_map.69
  25.8 16.0 %all_to_all.42 = f32[32,1,2176]{2,1,0:T(1,128)S(1)} all-to-all(f32[32,1,2176]{2,1,0:T(1,128)S(1)} %bitcast.28), channel_id=1, replica_groups=mesh['af'=32,'vert'=8] {'af'}, dimensions={0} | all-to-all | bytes 557056 | tf_op jit(solution)/shard_map/all_to_all | solution.py:276
  41.7 1.5 %shard_map.70 = (f32[544,128]{1,0:T(8,128)S(1)}, f32[8,8,192]{2,1,0:T(8,128)S(1)}, f32[8,128]{1,0:T(8,128)S(1)}) custom-call(f32[544,128]{1,0:T(8,128)S(1)} %bitcast.21, bf16[8,192,512]{2,1,0:T(8,128)(2,1)S(1)} %get-tuple-element.19.khi_ref, bf16[8,192,512]{2,1,0:T(8,128)(2,1)S(1)} %get-tuple-element.20.klo_ref, f32[8,8,192]{2,1,0:T(8,128)S(1)} %copy-done.1, ...), custom_call_target="tpu_custom_call" | custom-call | tf_op jit(solution)/shard_map/pallas_call | solution.py:264
  43.2 15.7 %all_to_all.43 = f32[32,1,2176]{2,1,0:T(1,128)S(1)} all-to-all(f32[32,1,2176]{2,1,0:T(1,128)S(1)} %bitcast.26), channel_id=1, replica_groups=mesh['af'=32,'vert'=8] {'af'}, dimensions={0} | all-to-all | bytes 557056 | tf_op jit(solution)/shard_map/all_to_all | solution.py:276
  58.9 0.8 shard_map.71
  59.7 14.9 %all_to_all.44 = f32[32,1,2176]{2,1,0:T(1,128)S(1)} all-to-all(f32[32,1,2176]{2,1,0:T(1,128)S(1)} %bitcast.27), channel_id=1, replica_groups=mesh['af'=32,'vert'=8] {'af'}, dimensions={0} | all-to-all | bytes 557056 | tf_op jit(solution)/shard_map/all_to_all | solution.py:276
  74.6 1.5 %shard_map.72 = (f32[544,128]{1,0:T(8,128)S(1)}, f32[8,8,192]{2,1,0:T(8,128)S(1)}, f32[8,128]{1,0:T(8,128)S(1)}) custom-call(f32[544,128]{1,0:T(8,128)S(1)} %bitcast.20, bf16[8,192,512]{2,1,0:T(8,128)(2,1)S(1)} %get-tuple-element.19.khi_ref, bf16[8,192,512]{2,1,0:T(8,128)(2,1)S(1)} %get-tuple-element.20.klo_ref, ...), custom_call_target="tpu_custom_call" | custom-call | tf_op jit(solution)/shard_map/pallas_call | solution.py:264
  76.0 14.2 %all_to_all.45 = f32[32,1,2176]{2,1,0:T(1,128)S(1)} all-to-all(f32[32,1,2176]{2,1,0:T(1,128)S(1)} %bitcast.25), channel_id=1, replica_groups=mesh['af'=32,'vert'=8] {'af'}, dimensions={0} | all-to-all | bytes 557056 | tf_op jit(solution)/shard_map/all_to_all | solution.py:276
  90.2 0.5 shard_map.73
  90.7 21.0 %all_to_all.46 = f32[32,1,6272]{2,1,0:T(1,128)S(1)} all-to-all(f32[32,1,6272]{2,1,0:T(1,128)S(1)} %bitcast.24), channel_id=1, replica_groups=mesh['af'=32,'vert'=8] {'af'}, dimensions={0} | all-to-all | bytes 1605632 | tf_op jit(solution)/shard_map/all_to_all | solution.py:276
  111.7 0.1 shard_map.74
  111.8 16.8 %all_to_all.47 = f32[8,8,128]{2,1,0:T(8,128)S(1)} all-to-all(f32[8,8,128]{2,1,0:T(8,128)S(1)} %bitcast.30), channel_id=1, replica_groups=mesh['af'=32,'vert'=8] {'vert'}, dimensions={0} | all-to-all | bytes 65536 | tf_op jit(solution)/shard_map/all_to_all | solution.py:326
  128.6 1.1 shard_map.75
Async XLA Ops:
  0.6 2.1 %copy-start.1 = (f32[8,8,192]{2,1,0:T(8,128)S(1)}, f32[8,8,192]{2,1,0:T(8,128)}, u32[]{:S(2)}) copy-start(f32[8,8,192]{2,1,0:T(8,128)} %q0_ref.1) | copy-start | bytes 147460
  2.7 22.3 %copy-start = (bf16[4,512,512]{2,1,0:T(8,128)(2,1)S(1)}, bf16[4,512,512]{2,1,0:T(8,128)(2,1)}, u32[]{:S(2)}) copy-start(bf16[4,512,512]{2,1,0:T(8,128)(2,1)} %constant.2.clone.refs_2_) | copy-start | bytes 6291460
  2.7 22.3 %copy-start.2 = (s32[512]{0:T(512)S(1)}, s32[512]{0:T(512)}, u32[]{:S(2)}) copy-start(s32[512]{0:T(512)} %param.6) | copy-start | bytes 6148

commit v5 on v4

--- a/solution.py
+++ b/solution.py
@@ -196,13 +196,20 @@
 def stats_kernel(recv, stats, out):
     total = arrived_sum(recv, LAST)
     row = lax.broadcasted_iota(jnp.int32, (8, 128), 0)
-    mine = jnp.where(row == 5, total, stats[...])
-    for g in range(VERT):
-        out[pl.ds(8 * g, 8), :] = mine
-
-
-def last_kernel(recv, gathered, q0_ref, q1_ref, q2_ref, sol_ref, dir_ref, left_ref, rows):
-    n0, m1, n1, m2, n2, m3 = [gathered[pl.ds(j, VERT, stride=8), :] for j in range(6)]
+    out[...] = jnp.where(row == 5, total, stats[...])
+
+
+def pair_kernel(mine, other, out):
+    out[pl.ds(0, 8), :] = mine[...]
+    out[pl.ds(8, 8), :] = other[...]
+
+
+def last_kernel(recv, g0, g1, g2, g3, q0_ref, q1_ref, q2_ref, sol_ref, dir_ref, left_ref, rows):
+    gathered = (g0, g1, g2, g3)
+    n0, m1, n1, m2, n2, m3 = [
+        jnp.concatenate([g[pl.ds(8 * c + j, 1), :] for g in gathered for c in range(2)], axis=0)
+        for j in range(6)
+    ]
 
     def norm(x):
         return jnp.sqrt(jnp.sum(x, axis=0, keepdims=True) + EPSILON)
@@ -246,7 +253,7 @@
     y3 = z3 / alpha3
     for j, value in enumerate((x1, x2, y1, y2, y3, c0, c1, c2)):
         rows[pl.ds(8 * j, 8), :] = jnp.broadcast_to(value, (VERT, 128))
-    group = lax.axis_index("vert")
+    group = 0
     x1, x2, y1, y2, y3, c0, c1, c2 = [rows[pl.ds(8 * j + group, 1), :] for j in range(8)]
     for v in range(VB):
         for q in range(QB):
@@ -322,14 +329,15 @@
         exchange(msg), cut, tables, stats, s1, s2,
     )
     arrived = exchange(msg)
-    [stats] = call(stats_kernel, [((VERT * 8, 128), F32)], arrived, stats)
-    gathered = lax.all_to_all(stats, "vert", split_axis=0, concat_axis=0, tiled=True)
+    [stats] = call(stats_kernel, [stat], arrived, stats)
+    [pair] = call(pair_kernel, [((16, 128), F32)], stats, lax.ppermute(stats, "vert", [(i, i ^ 1) for i in range(VERT)]))
+    gathered = [pair] + [lax.ppermute(pair, "vert", [(i, i ^ (2 * d)) for i in range(VERT)]) for d in (1, 2, 3)]
     out = ((VB, TB, RECV), F32)
     return tuple(
         call(
             last_kernel,
             [out, out, data],
-            arrived, gathered, recorded, q1, q2,
+            arrived, *gathered, recorded, q1, q2,
             scratch=[pltpu.VMEM((64, 128), F32)],
         )
     )

time: 130 us -> 128 us (0.985)
  blocking collectives: 120 us -> 103 us
  starting transfers between devices: 0 us -> 11.3 us
  waiting for transfers between devices: 0 us -> 3.65 us
    all_to_all x1 -> x0, blocking collectives: 16.8 us -> none  [per_device(): lax.all_to_all(stats, 'vert', split_axis=0, concat_axis=0, tiled=True)]
    ppermute x0 -> x4, starting transfers between devices: none -> 11.3 us  [the longest x1 8.04 us: per_device(): lax.ppermute(stats, 'vert', [(i, i ^ 1) for i in range(VERT)])]
    ppermute x0 -> x4, waiting for transfers between devices: none -> 3.65 us  [the longest x3 2.83 us: per_device(): lax.ppermute(pair, 'vert', [(i, i ^ 2 * d) for i in range(VERT)])]
    pallas_call x9 -> x10, Pallas kernels: 8.88 us -> 8.89 us  [call(): pl.pallas_call(body, out_shape=[jax.ShapeDtypeStruct(s, t) for s, t in ou...]
  transfers between devices with their start and end apart: 0 -> 4, of which waited for: 0 -> 3; matrix products, arithmetic and copies ran while one was open for 0% -> 0% of each run, Pallas kernels for 0% -> 0%
where the time goes in v5:
time: 128 us
  blocking collectives  103 us (80%)
  starting transfers between devices  11.3 us (9%)
  Pallas kernels  8.89 us (7%)
  waiting for transfers between devices  3.65 us (3%)
    all_to_all x6, blocking collectives, exchange(): flat = lax.all_to_all(flat, 'af', split_axis=0, concat_axis=0, tiled=True)  103 us
    pallas_call x10, Pallas kernels, call(): pl.pallas_call(body, out_shape=[jax.ShapeDtypeStruct(s, t) for s, t in ou...  8.89 us
    ppermute x1, starting transfers between devices, per_device(): lax.ppermute(stats, 'vert', [(i, i ^ 1) for i in range(VERT)])  8.04 us
    ppermute x3, starting transfers between devices, per_device(): lax.ppermute(pair, 'vert', [(i, i ^ 2 * d) for i in range(VERT)])  3.25 us
    ppermute x3, waiting for transfers between devices, per_device(): lax.ppermute(pair, 'vert', [(i, i ^ 2 * d) for i in range(VERT)])  2.83 us
  transfers between devices with their start and end apart: 4, of which 3 were waited for; matrix products, arithmetic and copies ran while one was open for 0% of the time, Pallas kernels for 0%

profile of v5, /device:TPU:1, one launch (start us, length us, event | category | flops | bytes accessed | tf_op | source)
XLA Modules:
  0.0 127.8 jit_solution(1172526422594912177)
XLA Ops:
  0.6 0.0 copy-start.1
  0.6 2.0 %shard_map.67 = (bf16[8,192,512]{2,1,0:T(8,128)(2,1)S(1)}, bf16[8,192,512]{2,1,0:T(8,128)(2,1)S(1)}) custom-call(f32[8,192,512]{2,1,0:T(8,128)} %bitcast.30), custom_call_target="tpu_custom_call" | custom-call | tf_op jit(solution)/shard_map/pallas_call | solution.py:271
  2.7 0.0 copy-start
  2.7 0.0 copy-start.2
  2.7 0.0 copy-done.1
  2.7 0.6 shard_map.68
  3.4 21.6 %all_to_all.30 = f32[32,1,2176]{2,1,0:T(1,128)S(1)} all-to-all(f32[32,1,2176]{2,1,0:T(1,128)S(1)} %bitcast.21), channel_id=1, replica_groups=mesh['af'=32,'vert'=8] {'af'}, dimensions={0} | all-to-all | bytes 557056 | tf_op jit(solution)/shard_map/all_to_all | solution.py:283
  25.0 0.0 copy-done
  25.0 0.0 copy-done.2
  25.0 0.8 shard_map.69
  25.8 16.0 %all_to_all.31 = f32[32,1,2176]{2,1,0:T(1,128)S(1)} all-to-all(f32[32,1,2176]{2,1,0:T(1,128)S(1)} %bitcast.26), channel_id=1, replica_groups=mesh['af'=32,'vert'=8] {'af'}, dimensions={0} | all-to-all | bytes 557056 | tf_op jit(solution)/shard_map/all_to_all | solution.py:283
  41.7 1.5 %shard_map.70 = (f32[544,128]{1,0:T(8,128)S(1)}, f32[8,8,192]{2,1,0:T(8,128)S(1)}, f32[8,128]{1,0:T(8,128)S(1)}) custom-call(f32[544,128]{1,0:T(8,128)S(1)} %bitcast.19, bf16[8,192,512]{2,1,0:T(8,128)(2,1)S(1)} %get-tuple-element.19.khi_ref, bf16[8,192,512]{2,1,0:T(8,128)(2,1)S(1)} %get-tuple-element.20.klo_ref, f32[8,8,192]{2,1,0:T(8,128)S(1)} %copy-done.1, ...), custom_call_target="tpu_custom_call" | custom-call | tf_op jit(solution)/shard_map/pallas_call | solution.py:271
  43.2 15.7 %all_to_all.32 = f32[32,1,2176]{2,1,0:T(1,128)S(1)} all-to-all(f32[32,1,2176]{2,1,0:T(1,128)S(1)} %bitcast.24), channel_id=1, replica_groups=mesh['af'=32,'vert'=8] {'af'}, dimensions={0} | all-to-all | bytes 557056 | tf_op jit(solution)/shard_map/all_to_all | solution.py:283
  58.9 0.8 shard_map.71
  59.7 14.9 %all_to_all.33 = f32[32,1,2176]{2,1,0:T(1,128)S(1)} all-to-all(f32[32,1,2176]{2,1,0:T(1,128)S(1)} %bitcast.25), channel_id=1, replica_groups=mesh['af'=32,'vert'=8] {'af'}, dimensions={0} | all-to-all | bytes 557056 | tf_op jit(solution)/shard_map/all_to_all | solution.py:283
  74.6 1.5 %shard_map.72 = (f32[544,128]{1,0:T(8,128)S(1)}, f32[8,8,192]{2,1,0:T(8,128)S(1)}, f32[8,128]{1,0:T(8,128)S(1)}) custom-call(f32[544,128]{1,0:T(8,128)S(1)} %bitcast.18, bf16[8,192,512]{2,1,0:T(8,128)(2,1)S(1)} %get-tuple-element.19.khi_ref, bf16[8,192,512]{2,1,0:T(8,128)(2,1)S(1)} %get-tuple-element.20.klo_ref, ...), custom_call_target="tpu_custom_call" | custom-call | tf_op jit(solution)/shard_map/pallas_call | solution.py:271
  76.0 14.2 %all_to_all.34 = f32[32,1,2176]{2,1,0:T(1,128)S(1)} all-to-all(f32[32,1,2176]{2,1,0:T(1,128)S(1)} %bitcast.23), channel_id=1, replica_groups=mesh['af'=32,'vert'=8] {'af'}, dimensions={0} | all-to-all | bytes 557056 | tf_op jit(solution)/shard_map/all_to_all | solution.py:283
  90.2 0.5 shard_map.73
  90.7 21.0 %all_to_all.35 = f32[32,1,6272]{2,1,0:T(1,128)S(1)} all-to-all(f32[32,1,6272]{2,1,0:T(1,128)S(1)} %bitcast.22), channel_id=1, replica_groups=mesh['af'=32,'vert'=8] {'af'}, dimensions={0} | all-to-all | bytes 1605632 | tf_op jit(solution)/shard_map/all_to_all | solution.py:283
  111.7 0.1 shard_map.74.mine
  111.8 8.0 %collective-permute-start = (f32[8,128]{1,0:T(8,128)S(1)}, f32[8,128]{1,0:T(8,128)S(1)}, u32[]{:S(2)}, u32[]{:S(2)}) collective-permute-start(f32[8,128]{1,0:T(8,128)S(1)} %shard_map.74.mine), channel_id=1, source_target_pairs={{0,1},{1,0},{2,3},{3,2},{4,5},{5,4},{6,7},{7,6},{8,9},{9,8},{10,11... | collective-permute-start | bytes 12296 | tf_op jit(solution)/shard_map/ppermute | solution.py:333
  119.8 0.8 collective-permute-done.other
  120.7 2.1 %collective-permute-start.3 = (f32[16,128]{1,0:T(8,128)S(1)}, f32[16,128]{1,0:T(8,128)S(1)}, u32[]{:S(2)}, u32[]{:S(2)}) collective-permute-start(f32[16,128]{1,0:T(8,128)S(1)} %shard_map.75.g0), channel_id=1, source_target_pairs={{0,6},{1,7},{2,4},{3,5},{4,2},{5,3},{6,0},{7,1},{8,14},{9,15},{10,... | collective-permute-start | bytes 24584 | tf_op jit(solution)/shard_map/ppermute | solution.py:334
  122.7 0.7 collective-permute-start.2
  123.4 0.5 collective-permute-start.1
  123.9 0.5 collective-permute-done.3.g3
  124.4 2.4 %collective-permute-done.2.g2 = f32[16,128]{1,0:T(8,128)S(1)} collective-permute-done((f32[16,128]{1,0:T(8,128)S(1)}, f32[16,128]{1,0:T(8,128)S(1)}, u32[]{:S(2)}, u32[]{:S(2)}) %collective-permute-start.2) | collective-permute-done | bytes 8224 | tf_op jit(solution)/shard_map/ppermute | solution.py:334
  126.7 0.0 collective-permute-done.1.g1
  126.8 1.1 shard_map.76
  (1 shorter events, 0.0 us)
Async XLA Ops:
  0.6 2.1 %copy-start.1 = (f32[8,8,192]{2,1,0:T(8,128)S(1)}, f32[8,8,192]{2,1,0:T(8,128)}, u32[]{:S(2)}) copy-start(f32[8,8,192]{2,1,0:T(8,128)} %q0_ref.1) | copy-start | bytes 147460
  2.7 22.3 %copy-start = (bf16[4,512,512]{2,1,0:T(8,128)(2,1)S(1)}, bf16[4,512,512]{2,1,0:T(8,128)(2,1)}, u32[]{:S(2)}) copy-start(bf16[4,512,512]{2,1,0:T(8,128)(2,1)} %constant.2.clone.refs_2_) | copy-start | bytes 6291460
  2.7 22.3 %copy-start.2 = (s32[512]{0:T(512)S(1)}, s32[512]{0:T(512)}, u32[]{:S(2)}) copy-start(s32[512]{0:T(512)} %param.6) | copy-start | bytes 6148
  111.8 8.9 %collective-permute-start = (f32[8,128]{1,0:T(8,128)S(1)}, f32[8,128]{1,0:T(8,128)S(1)}, u32[]{:S(2)}, u32[]{:S(2)}) collective-permute-start(f32[8,128]{1,0:T(8,128)S(1)} %shard_map.74.mine), channel_id=1, source_target_pairs={{0,1},{1,0},{2,3},{3,2},{4,5},{5,4},{6,7},{7,6},{8,9},{9,8},{10,11... | collective-permute-start | bytes 12296 | tf_op jit(solution)/shard_map/ppermute | solution.py:333
  120.7 3.7 %collective-permute-start.3 = (f32[16,128]{1,0:T(8,128)S(1)}, f32[16,128]{1,0:T(8,128)S(1)}, u32[]{:S(2)}, u32[]{:S(2)}) collective-permute-start(f32[16,128]{1,0:T(8,128)S(1)} %shard_map.75.g0), channel_id=1, source_target_pairs={{0,6},{1,7},{2,4},{3,5},{4,2},{5,3},{6,0},{7,1},{8,14},{9,15},{10,... | collective-permute-start | bytes 24584 | tf_op jit(solution)/shard_map/ppermute | solution.py:334
  122.7 4.0 %collective-permute-start.2 = (f32[16,128]{1,0:T(8,128)S(1)}, f32[16,128]{1,0:T(8,128)S(1)}, u32[]{:S(2)}, u32[]{:S(2)}) collective-permute-start(f32[16,128]{1,0:T(8,128)S(1)} %shard_map.75.g0), channel_id=1, source_target_pairs={{0,4},{1,5},{2,6},{3,7},{4,0},{5,1},{6,2},{7,3},{8,12},{9,13},{10,... | collective-permute-start | bytes 24584 | tf_op jit(solution)/shard_map/ppermute | solution.py:334
  123.4 3.3 %collective-permute-start.1 = (f32[16,128]{1,0:T(8,128)S(1)}, f32[16,128]{1,0:T(8,128)S(1)}, u32[]{:S(2)}, u32[]{:S(2)}) collective-permute-start(f32[16,128]{1,0:T(8,128)S(1)} %shard_map.75.g0), channel_id=1, source_target_pairs={{0,2},{1,3},{2,0},{3,1},{4,6},{5,7},{6,4},{7,5},{8,10},{9,11},{10,... | collective-permute-start | bytes 24584 | tf_op jit(solution)/shard_map/ppermute | solution.py:334

commit v6 on v5

--- a/solution.py
+++ b/solution.py
@@ -66,11 +66,15 @@
     return both[: 2 * VB] + both[2 * VB :] + dot(hi, klo)
 
 
-def kernel_forward(x, khi, klo):
+def kernel_forward(x, khi, klo, product):
     hi, lo = split(x)
-    both = dot_nt(jnp.concatenate([hi, lo], axis=0), khi)
-    y = both[: 2 * VB] + both[2 * VB :] + dot_nt(hi, klo)
+    both = product(jnp.concatenate([hi, lo], axis=0), khi)
+    y = both[: 2 * VB] + both[2 * VB :] + product(hi, klo)
     return y[:VB] + turned(y[VB:], -1.0)
+
+
+def on_core(core):
+    return lax.rem(lax.axis_index("vert"), 2) == core
 
 
 def ratio(a, b):
@@ -113,7 +117,7 @@
             khi_ref[f], klo_ref[f] = split(k_buf[f])
 
 
-def first_kernel(u_ref, khi_ref, klo_ref, msg):
+def first_kernel(u_ref, khi_ref, klo_ref, msg, thi_ref, tlo_ref):
     square = jnp.zeros((VB, 2 * SRCS), F32)
     for f in range(FB):
         u = u_ref[f]
@@ -121,35 +125,48 @@
         put_spectra(msg, f, kernel_adjoint(u, khi_ref[f], klo_ref[f]))
     put_partial(msg, lane_zero(jnp.sum(square, keepdims=True)), MSG)
 
-
-def data_kernel(order, recv, khi_ref, klo_ref, before_ref, stats, msg, q_ref, stats_out):
+    @pl.when(on_core(0))
+    def _():
+        for f in range(FB):
+            thi_ref[f] = khi_ref[f].T
+            tlo_ref[f] = klo_ref[f].T
+
+
+def data_kernel(
+    order, recv, khi_ref, klo_ref, thi_ref, tlo_ref, before_ref, stats, msg, q_ref, stats_out
+):
     total = arrived_sum(recv, MSG)
     stats_out[...] = stats[...]
     stats_out[pl.ds(order, 1), :] = total
     coefficient = ratio(total, stats[pl.ds(order - 1, 1), :])[:, :1]
-    square = jnp.zeros((VB, 2 * SRCS), F32)
-    steps = []
-    for f in range(FB):
-        x = jnp.concatenate(
-            [
-                jnp.concatenate(
-                    [
-                        recv[pl.ds(q * MSG + 2 * f + c, VB, stride=QB * MSG), :]
-                        for q in range(QB)
-                    ],
-                    axis=1,
-                )
-                for c in range(2)
-            ],
-            axis=0,
-        )
-        u = kernel_forward(x, khi_ref[f], klo_ref[f]) - coefficient * before_ref[f]
-        q_ref[f] = u
-        square += u * u
-        steps.append(u)
-    for f in range(FB):
-        put_spectra(msg, f, kernel_adjoint(steps[f], khi_ref[f], klo_ref[f]))
-    put_partial(msg, lane_zero(jnp.sum(square, keepdims=True)), MSG)
+
+    def step(hi_ref, lo_ref, product):
+        square = jnp.zeros((VB, 2 * SRCS), F32)
+        steps = []
+        for f in range(FB):
+            x = jnp.concatenate(
+                [
+                    jnp.concatenate(
+                        [
+                            recv[pl.ds(q * MSG + 2 * f + c, VB, stride=QB * MSG), :]
+                            for q in range(QB)
+                        ],
+                        axis=1,
+                    )
+                    for c in range(2)
+                ],
+                axis=0,
+            )
+            u = kernel_forward(x, hi_ref[f], lo_ref[f], product) - coefficient * before_ref[f]
+            q_ref[f] = u
+            square += u * u
+            steps.append(u)
+        for f in range(FB):
+            put_spectra(msg, f, kernel_adjoint(steps[f], khi_ref[f], klo_ref[f]))
+        put_partial(msg, lane_zero(jnp.sum(square, keepdims=True)), MSG)
+
+    pl.when(on_core(0))(lambda: step(thi_ref, tlo_ref, dot))
+    pl.when(on_core(1))(lambda: step(khi_ref, klo_ref, dot_nt))
 
 
 def table_apply(table_ref, at, x):
@@ -302,7 +319,10 @@
         space=pltpu.HBM,
         vmem=49,
     )
-    [msg] = call(first_kernel, [message], recorded, khi, klo)
+    turned_halves = ((FB, RECV, 2 * SRCS), BF16)
+    msg, thi, tlo = call(
+        first_kernel, [message, turned_halves, turned_halves], recorded, khi, klo
+    )
     msg, s1, stats = call(
         functools.partial(model_kernel, 0, False),
         [message, model, stat],
@@ -311,7 +331,7 @@
     msg, q1, stats = call(
         functools.partial(data_kernel, 1),
         [message, data, stat],
-        exchange(msg), khi, klo, recorded, stats,
+        exchange(msg), khi, klo, thi, tlo, recorded, stats,
     )
     msg, s2, stats = call(
         functools.partial(model_kernel, 2, False),
@@ -321,7 +341,7 @@
     msg, q2, stats = call(
         functools.partial(data_kernel, 3),
         [message, data, stat],
-        exchange(msg), khi, klo, q1, stats,
+        exchange(msg), khi, klo, thi, tlo, q1, stats,
     )
     msg, stats = call(
         functools.partial(model_kernel, 4, True),

time: 128 us -> 126 us (0.984)
  blocking collectives: 103 us -> 98.6 us
  starting transfers between devices: 11.3 us -> 12.9 us
    all_to_all x6, blocking collectives: 103 us -> 98.6 us  [exchange(): flat = lax.all_to_all(flat, 'af', split_axis=0, concat_axis=0, tiled=True)]
    ppermute x1, starting transfers between devices: 8.04 us -> 9.67 us  [per_device(): lax.ppermute(stats, 'vert', [(i, i ^ 1) for i in range(VERT)])]
where the time goes in v6:
time: 126 us; the launch traced here: 125 us
  blocking collectives  98.6 us (78%)
  starting transfers between devices  12.9 us (10%)
  Pallas kernels  9.12 us (7%)
  waiting for transfers between devices  4.06 us (3%)
    all_to_all x6, blocking collectives, exchange(): flat = lax.all_to_all(flat, 'af', split_axis=0, concat_axis=0, tiled=True)  98.6 us
    ppermute x1, starting transfers between devices, per_device(): lax.ppermute(stats, 'vert', [(i, i ^ 1) for i in range(VERT)])  9.67 us
    pallas_call x10, Pallas kernels, call(): pl.pallas_call(body, out_shape=[jax.ShapeDtypeStruct(s, t) for s, t in ou...  9.12 us
    ppermute x3, starting transfers between devices, per_device(): lax.ppermute(pair, 'vert', [(i, i ^ 2 * d) for i in range(VERT)])  3.25 us
    ppermute x3, waiting for transfers between devices, per_device(): lax.ppermute(pair, 'vert', [(i, i ^ 2 * d) for i in range(VERT)])  3.23 us
  transfers between devices with their start and end apart: 4, of which 3 were waited for; matrix products, arithmetic and copies ran while one was open for 0% of the time, Pallas kernels for 0%

profile of v6, /device:TPU:1, one launch (start us, length us, event | category | flops | bytes accessed | tf_op | source)
XLA Modules:
  0.0 125.5 jit_solution(12771591921876019586)
XLA Ops:
  0.6 0.0 copy-start.1
  0.6 2.0 %shard_map.67 = (bf16[8,192,512]{2,1,0:T(8,128)(2,1)S(1)}, bf16[8,192,512]{2,1,0:T(8,128)(2,1)S(1)}) custom-call(f32[8,192,512]{2,1,0:T(8,128)} %bitcast.30), custom_call_target="tpu_custom_call" | custom-call | tf_op jit(solution)/shard_map/pallas_call | solution.py:288
  2.7 0.0 copy-start
  2.7 0.0 copy-start.2
  2.7 0.0 copy-done.1
  2.7 0.6 shard_map.68
  3.4 21.6 %all_to_all.30 = f32[32,1,2176]{2,1,0:T(1,128)S(1)} all-to-all(f32[32,1,2176]{2,1,0:T(1,128)S(1)} %bitcast.26), channel_id=1, replica_groups=mesh['af'=32,'vert'=8] {'af'}, dimensions={0} | all-to-all | bytes 557056 | tf_op jit(solution)/shard_map/all_to_all | solution.py:300
  24.9 0.0 copy-done
  25.0 0.0 copy-done.2
  25.0 0.8 shard_map.69
  25.8 15.2 %all_to_all.31 = f32[32,1,2176]{2,1,0:T(1,128)S(1)} all-to-all(f32[32,1,2176]{2,1,0:T(1,128)S(1)} %bitcast.25), channel_id=1, replica_groups=mesh['af'=32,'vert'=8] {'af'}, dimensions={0} | all-to-all | bytes 557056 | tf_op jit(solution)/shard_map/all_to_all | solution.py:300
  40.9 1.6 %shard_map.70 = (f32[544,128]{1,0:T(8,128)S(1)}, f32[8,8,192]{2,1,0:T(8,128)S(1)}, f32[8,128]{1,0:T(8,128)S(1)}) custom-call(f32[544,128]{1,0:T(8,128)S(1)} %bitcast.18, bf16[8,192,512]{2,1,0:T(8,128)(2,1)S(1)} %get-tuple-element.22.khi_ref, bf16[8,192,512]{2,1,0:T(8,128)(2,1)S(1)} %get-tuple-element.23.klo_ref, ...), custom_call_target="tpu_custom_call" | custom-call | tf_op jit(solution)/shard_map/pallas_call | solution.py:288
  42.5 14.4 %all_to_all.32 = f32[32,1,2176]{2,1,0:T(1,128)S(1)} all-to-all(f32[32,1,2176]{2,1,0:T(1,128)S(1)} %bitcast.23), channel_id=1, replica_groups=mesh['af'=32,'vert'=8] {'af'}, dimensions={0} | all-to-all | bytes 557056 | tf_op jit(solution)/shard_map/all_to_all | solution.py:300
  56.9 0.8 shard_map.71
  57.7 14.1 %all_to_all.33 = f32[32,1,2176]{2,1,0:T(1,128)S(1)} all-to-all(f32[32,1,2176]{2,1,0:T(1,128)S(1)} %bitcast.24), channel_id=1, replica_groups=mesh['af'=32,'vert'=8] {'af'}, dimensions={0} | all-to-all | bytes 557056 | tf_op jit(solution)/shard_map/all_to_all | solution.py:300
  71.8 1.6 %shard_map.72 = (f32[544,128]{1,0:T(8,128)S(1)}, f32[8,8,192]{2,1,0:T(8,128)S(1)}, f32[8,128]{1,0:T(8,128)S(1)}) custom-call(f32[544,128]{1,0:T(8,128)S(1)} %bitcast.16, bf16[8,192,512]{2,1,0:T(8,128)(2,1)S(1)} %get-tuple-element.22.khi_ref, bf16[8,192,512]{2,1,0:T(8,128)(2,1)S(1)} %get-tuple-element.23.klo_ref, ...), custom_call_target="tpu_custom_call" | custom-call | tf_op jit(solution)/shard_map/pallas_call | solution.py:288
  73.4 14.1 %all_to_all.34 = f32[32,1,2176]{2,1,0:T(1,128)S(1)} all-to-all(f32[32,1,2176]{2,1,0:T(1,128)S(1)} %bitcast.22), channel_id=1, replica_groups=mesh['af'=32,'vert'=8] {'af'}, dimensions={0} | all-to-all | bytes 557056 | tf_op jit(solution)/shard_map/all_to_all | solution.py:300
  87.5 0.5 shard_map.73
  88.0 19.3 %all_to_all.35 = f32[32,1,6272]{2,1,0:T(1,128)S(1)} all-to-all(f32[32,1,6272]{2,1,0:T(1,128)S(1)} %bitcast.21), channel_id=1, replica_groups=mesh['af'=32,'vert'=8] {'af'}, dimensions={0} | all-to-all | bytes 1605632 | tf_op jit(solution)/shard_map/all_to_all | solution.py:300
  107.3 0.1 shard_map.74.mine
  107.4 9.7 %collective-permute-start = (f32[8,128]{1,0:T(8,128)S(1)}, f32[8,128]{1,0:T(8,128)S(1)}, u32[]{:S(2)}, u32[]{:S(2)}) collective-permute-start(f32[8,128]{1,0:T(8,128)S(1)} %shard_map.74.mine), channel_id=1, source_target_pairs={{0,1},{1,0},{2,3},{3,2},{4,5},{5,4},{6,7},{7,6},{8,9},{9,8},{10,11... | collective-permute-start | bytes 12296 | tf_op jit(solution)/shard_map/ppermute | solution.py:353
  117.1 0.8 collective-permute-done.other
  117.9 2.5 %collective-permute-start.3 = (f32[16,128]{1,0:T(8,128)S(1)}, f32[16,128]{1,0:T(8,128)S(1)}, u32[]{:S(2)}, u32[]{:S(2)}) collective-permute-start(f32[16,128]{1,0:T(8,128)S(1)} %shard_map.75.g0), channel_id=1, source_target_pairs={{0,6},{1,7},{2,4},{3,5},{4,2},{5,3},{6,0},{7,1},{8,14},{9,15},{10,... | collective-permute-start | bytes 24584 | tf_op jit(solution)/shard_map/ppermute | solution.py:354
  120.4 0.5 collective-permute-start.2
  120.9 0.3 collective-permute-start.1
  121.2 0.5 collective-permute-done.3.g3
  121.6 2.8 %collective-permute-done.2.g2 = f32[16,128]{1,0:T(8,128)S(1)} collective-permute-done((f32[16,128]{1,0:T(8,128)S(1)}, f32[16,128]{1,0:T(8,128)S(1)}, u32[]{:S(2)}, u32[]{:S(2)}) %collective-permute-start.2) | collective-permute-done | bytes 8224 | tf_op jit(solution)/shard_map/ppermute | solution.py:354
  124.4 0.0 collective-permute-done.1.g1
  124.4 1.1 shard_map.76
  (1 shorter events, 0.0 us)
Async XLA Ops:
  0.6 2.1 %copy-start.1 = (f32[8,8,192]{2,1,0:T(8,128)S(1)}, f32[8,8,192]{2,1,0:T(8,128)}, u32[]{:S(2)}) copy-start(f32[8,8,192]{2,1,0:T(8,128)} %q0_ref.1) | copy-start | bytes 147460
  2.7 22.3 %copy-start = (bf16[4,512,512]{2,1,0:T(8,128)(2,1)S(1)}, bf16[4,512,512]{2,1,0:T(8,128)(2,1)}, u32[]{:S(2)}) copy-start(bf16[4,512,512]{2,1,0:T(8,128)(2,1)} %constant.2.clone.refs_2_) | copy-start | bytes 6291460
  2.7 22.3 %copy-start.2 = (s32[512]{0:T(512)S(1)}, s32[512]{0:T(512)}, u32[]{:S(2)}) copy-start(s32[512]{0:T(512)} %param.6) | copy-start | bytes 6148
  107.4 10.5 %collective-permute-start = (f32[8,128]{1,0:T(8,128)S(1)}, f32[8,128]{1,0:T(8,128)S(1)}, u32[]{:S(2)}, u32[]{:S(2)}) collective-permute-start(f32[8,128]{1,0:T(8,128)S(1)} %shard_map.74.mine), channel_id=1, source_target_pairs={{0,1},{1,0},{2,3},{3,2},{4,5},{5,4},{6,7},{7,6},{8,9},{9,8},{10,11... | collective-permute-start | bytes 12296 | tf_op jit(solution)/shard_map/ppermute | solution.py:353
  117.9 3.7 %collective-permute-start.3 = (f32[16,128]{1,0:T(8,128)S(1)}, f32[16,128]{1,0:T(8,128)S(1)}, u32[]{:S(2)}, u32[]{:S(2)}) collective-permute-start(f32[16,128]{1,0:T(8,128)S(1)} %shard_map.75.g0), channel_id=1, source_target_pairs={{0,6},{1,7},{2,4},{3,5},{4,2},{5,3},{6,0},{7,1},{8,14},{9,15},{10,... | collective-permute-start | bytes 24584 | tf_op jit(solution)/shard_map/ppermute | solution.py:354
  120.4 4.0 %collective-permute-start.2 = (f32[16,128]{1,0:T(8,128)S(1)}, f32[16,128]{1,0:T(8,128)S(1)}, u32[]{:S(2)}, u32[]{:S(2)}) collective-permute-start(f32[16,128]{1,0:T(8,128)S(1)} %shard_map.75.g0), channel_id=1, source_target_pairs={{0,4},{1,5},{2,6},{3,7},{4,0},{5,1},{6,2},{7,3},{8,12},{9,13},{10,... | collective-permute-start | bytes 24584 | tf_op jit(solution)/shard_map/ppermute | solution.py:354
  120.9 3.5 %collective-permute-start.1 = (f32[16,128]{1,0:T(8,128)S(1)}, f32[16,128]{1,0:T(8,128)S(1)}, u32[]{:S(2)}, u32[]{:S(2)}) collective-permute-start(f32[16,128]{1,0:T(8,128)S(1)} %shard_map.75.g0), channel_id=1, source_target_pairs={{0,2},{1,3},{2,0},{3,1},{4,6},{5,7},{6,4},{7,5},{8,10},{9,11},{10,... | collective-permute-start | bytes 24584 | tf_op jit(solution)/shard_map/ppermute | solution.py:354

commit v7 on v6

--- a/solution.py
+++ b/solution.py
@@ -91,10 +91,10 @@
     return jnp.where(lane == 0, jnp.broadcast_to(total, (1, 128)), 0.0)
 
 
-def put_spectra(msg, f, z):
+def put_spectra(msg, f, z, pitch):
     for c in range(2):
         for q in range(QB):
-            msg[pl.ds(q * MSG + 2 * f + c, VB, stride=QB * MSG), :] = z[
+            msg[pl.ds(q * pitch + 2 * f + c, VB, stride=QB * pitch), :] = z[
                 c * VB : (c + 1) * VB, q * 128 : (q + 1) * 128
             ]
 
@@ -117,13 +117,13 @@
             khi_ref[f], klo_ref[f] = split(k_buf[f])
 
 
-def first_kernel(u_ref, khi_ref, klo_ref, msg, thi_ref, tlo_ref):
+def first_kernel(u_ref, khi_ref, klo_ref, msg, square_ref, thi_ref, tlo_ref):
     square = jnp.zeros((VB, 2 * SRCS), F32)
     for f in range(FB):
         u = u_ref[f]
         square += u * u
-        put_spectra(msg, f, kernel_adjoint(u, khi_ref[f], klo_ref[f]))
-    put_partial(msg, lane_zero(jnp.sum(square, keepdims=True)), MSG)
+        put_spectra(msg, f, kernel_adjoint(u, khi_ref[f], klo_ref[f]), KB)
+    square_ref[...] = jnp.broadcast_to(jnp.sum(square, keepdims=True), (1, 128))
 
     @pl.when(on_core(0))
     def _():
@@ -135,10 +135,21 @@
 def data_kernel(
     order, recv, khi_ref, klo_ref, thi_ref, tlo_ref, before_ref, stats, msg, q_ref, stats_out
 ):
-    total = arrived_sum(recv, MSG)
-    stats_out[...] = stats[...]
+    if order == 1:
+        rows = jnp.sum(recv[pl.ds(KB, AF, stride=MSG), :], axis=0, keepdims=True)
+        low = lax.broadcasted_iota(jnp.int32, (1, 128), 1) < 64
+        total, first = [
+            jnp.broadcast_to(jnp.sum(jnp.where(half, rows, 0.0), keepdims=True), (1, 128))
+            for half in (low, ~low)
+        ]
+        stats_out[...] = jnp.zeros((8, 128), F32)
+        stats_out[pl.ds(0, 1), :] = first
+    else:
+        total = arrived_sum(recv, MSG)
+        first = stats[pl.ds(order - 1, 1), :]
+        stats_out[...] = stats[...]
     stats_out[pl.ds(order, 1), :] = total
-    coefficient = ratio(total, stats[pl.ds(order - 1, 1), :])[:, :1]
+    coefficient = ratio(total, first)[:, :1]
 
     def step(hi_ref, lo_ref, product):
         square = jnp.zeros((VB, 2 * SRCS), F32)
@@ -162,7 +173,7 @@
             square += u * u
             steps.append(u)
         for f in range(FB):
-            put_spectra(msg, f, kernel_adjoint(steps[f], khi_ref[f], klo_ref[f]))
+            put_spectra(msg, f, kernel_adjoint(steps[f], khi_ref[f], klo_ref[f]), MSG)
         put_partial(msg, lane_zero(jnp.sum(square, keepdims=True)), MSG)
 
     pl.when(on_core(0))(lambda: step(thi_ref, tlo_ref, dot))
@@ -179,11 +190,13 @@
     refs = list(refs)
     recv, cut_ref, table_ref = refs[:3]
     refs = refs[3:]
+    stats = refs.pop(0)
     if order > 0:
-        stats = refs.pop(0)
         earlier = [refs.pop(0) for _ in range(order // 2)]
-    total = arrived_sum(recv, MSG)
-    spectra = jnp.concatenate([recv[pl.ds(p * MSG, KB), :] for p in range(AF)], axis=0)
+        total = arrived_sum(recv, MSG)
+        spectra = jnp.concatenate([recv[pl.ds(p * MSG, KB), :] for p in range(AF)], axis=0)
+    else:
+        spectra = recv[...]
     s = table_apply(table_ref, 0, spectra)
     if order > 0:
         s = s - ratio(total, stats[pl.ds(order - 1, 1), :]) * earlier[-1][...]
@@ -191,13 +204,18 @@
     keep = lax.broadcasted_iota(jnp.int32, (SAMPLES, 128), 0) < cut
     s = jnp.where(keep, s, 0.0)
     partial = jnp.sum(s * s, axis=0, keepdims=True)
-    if last:
-        msg, stats_out = refs
-    else:
-        msg, s_ref, stats_out = refs
+    if order == 0:
+        lane = lax.broadcasted_iota(jnp.int32, (1, 128), 1)
+        whole = jnp.broadcast_to(jnp.sum(partial, keepdims=True), (1, 128))
+        partial = jnp.where(lane == 0, whole, jnp.where(lane == 64, stats[...], 0.0))
+    msg = refs.pop(0)
+    if not last:
+        s_ref = refs.pop(0)
         s_ref[...] = s
-    stats_out[...] = stats[...] if order > 0 else jnp.zeros((8, 128), F32)
-    stats_out[pl.ds(order, 1), :] = total
+    if order > 0:
+        [stats_out] = refs
+        stats_out[...] = stats[...]
+        stats_out[pl.ds(order, 1), :] = total
     if last:
         for j, value in enumerate([e[...] for e in earlier] + [s]):
             for p in range(AF):
@@ -320,18 +338,20 @@
         vmem=49,
     )
     turned_halves = ((FB, RECV, 2 * SRCS), BF16)
-    msg, thi, tlo = call(
-        first_kernel, [message, turned_halves, turned_halves], recorded, khi, klo
-    )
-    msg, s1, stats = call(
+    msg, square, thi, tlo = call(
+        first_kernel,
+        [((AF * KB, 128), F32), ((1, 128), F32), turned_halves, turned_halves],
+        recorded, khi, klo,
+    )
+    msg, s1 = call(
         functools.partial(model_kernel, 0, False),
-        [message, model, stat],
-        exchange(msg), cut, tables,
+        [message, model],
+        exchange(msg), cut, tables, square,
     )
     msg, q1, stats = call(
         functools.partial(data_kernel, 1),
         [message, data, stat],
-        exchange(msg), khi, klo, thi, tlo, recorded, stats,
+        exchange(msg), khi, klo, thi, tlo, recorded, square,
     )
     msg, s2, stats = call(
         functools.partial(model_kernel, 2, False),

time: 126 us -> 125 us (level)
  no operation moved by 1% of the time
where the time goes in v7:
time: 125 us
  blocking collectives  97.9 us (78%)
  starting transfers between devices  13.2 us (11%)
  Pallas kernels  9.19 us (7%)
  waiting for transfers between devices  4.05 us (3%)
    all_to_all x6, blocking collectives, exchange(): flat = lax.all_to_all(flat, 'af', split_axis=0, concat_axis=0, tiled=True)  97.9 us
    ppermute x1, starting transfers between devices, per_device(): lax.ppermute(stats, 'vert', [(i, i ^ 1) for i in range(VERT)])  9.92 us
    pallas_call x10, Pallas kernels, call(): pl.pallas_call(body, out_shape=[jax.ShapeDtypeStruct(s, t) for s, t in ou...  9.19 us
    ppermute x3, starting transfers between devices, per_device(): lax.ppermute(pair, 'vert', [(i, i ^ 2 * d) for i in range(VERT)])  3.25 us
    ppermute x3, waiting for transfers between devices, per_device(): lax.ppermute(pair, 'vert', [(i, i ^ 2 * d) for i in range(VERT)])  3.23 us
  transfers between devices with their start and end apart: 4, of which 3 were waited for; matrix products, arithmetic and copies ran while one was open for 0% of the time, Pallas kernels for 0%

profile of v7, /device:TPU:1, one launch (start us, length us, event | category | flops | bytes accessed | tf_op | source)
XLA Modules:
  0.0 125.1 jit_solution(15930808030451679019)
XLA Ops:
  0.6 0.0 copy-start.1
  0.6 2.0 %shard_map.67 = (bf16[8,192,512]{2,1,0:T(8,128)(2,1)S(1)}, bf16[8,192,512]{2,1,0:T(8,128)(2,1)S(1)}) custom-call(f32[8,192,512]{2,1,0:T(8,128)} %bitcast.30), custom_call_target="tpu_custom_call" | custom-call | tf_op jit(solution)/shard_map/pallas_call | solution.py:306
  2.7 0.0 copy-start
  2.7 0.0 copy-start.2
  2.7 0.0 copy-done.1
  2.7 0.7 shard_map.68
  3.4 21.5 %all_to_all.30 = f32[32,1,2048]{2,1,0:T(1,128)S(1)} all-to-all(f32[32,1,2048]{2,1,0:T(1,128)S(1)} %bitcast.26), channel_id=1, replica_groups=mesh['af'=32,'vert'=8] {'af'}, dimensions={0} | all-to-all | bytes 524288 | tf_op jit(solution)/shard_map/all_to_all | solution.py:318
  24.9 0.0 copy-done
  24.9 0.0 copy-done.2
  24.9 0.8 shard_map.69
  25.7 14.7 %all_to_all.31 = f32[32,1,2176]{2,1,0:T(1,128)S(1)} all-to-all(f32[32,1,2176]{2,1,0:T(1,128)S(1)} %bitcast.25), channel_id=1, replica_groups=mesh['af'=32,'vert'=8] {'af'}, dimensions={0} | all-to-all | bytes 557056 | tf_op jit(solution)/shard_map/all_to_all | solution.py:318
  40.5 1.6 %shard_map.70 = (f32[544,128]{1,0:T(8,128)S(1)}, f32[8,8,192]{2,1,0:T(8,128)S(1)}, f32[8,128]{1,0:T(8,128)S(1)}) custom-call(f32[544,128]{1,0:T(8,128)S(1)} %bitcast.18, bf16[8,192,512]{2,1,0:T(8,128)(2,1)S(1)} %get-tuple-element.22.khi_ref, bf16[8,192,512]{2,1,0:T(8,128)(2,1)S(1)} %get-tuple-element.23.klo_ref, ...), custom_call_target="tpu_custom_call" | custom-call | tf_op jit(solution)/shard_map/pallas_call | solution.py:306
  42.1 14.3 %all_to_all.32 = f32[32,1,2176]{2,1,0:T(1,128)S(1)} all-to-all(f32[32,1,2176]{2,1,0:T(1,128)S(1)} %bitcast.23), channel_id=1, replica_groups=mesh['af'=32,'vert'=8] {'af'}, dimensions={0} | all-to-all | bytes 557056 | tf_op jit(solution)/shard_map/all_to_all | solution.py:318
  56.4 0.8 shard_map.71
  57.2 14.1 %all_to_all.33 = f32[32,1,2176]{2,1,0:T(1,128)S(1)} all-to-all(f32[32,1,2176]{2,1,0:T(1,128)S(1)} %bitcast.24), channel_id=1, replica_groups=mesh['af'=32,'vert'=8] {'af'}, dimensions={0} | all-to-all | bytes 557056 | tf_op jit(solution)/shard_map/all_to_all | solution.py:318
  71.3 1.6 %shard_map.72 = (f32[544,128]{1,0:T(8,128)S(1)}, f32[8,8,192]{2,1,0:T(8,128)S(1)}, f32[8,128]{1,0:T(8,128)S(1)}) custom-call(f32[544,128]{1,0:T(8,128)S(1)} %bitcast.16, bf16[8,192,512]{2,1,0:T(8,128)(2,1)S(1)} %get-tuple-element.22.khi_ref, bf16[8,192,512]{2,1,0:T(8,128)(2,1)S(1)} %get-tuple-element.23.klo_ref, ...), custom_call_target="tpu_custom_call" | custom-call | tf_op jit(solution)/shard_map/pallas_call | solution.py:306
  72.9 14.1 %all_to_all.34 = f32[32,1,2176]{2,1,0:T(1,128)S(1)} all-to-all(f32[32,1,2176]{2,1,0:T(1,128)S(1)} %bitcast.22), channel_id=1, replica_groups=mesh['af'=32,'vert'=8] {'af'}, dimensions={0} | all-to-all | bytes 557056 | tf_op jit(solution)/shard_map/all_to_all | solution.py:318
  87.0 0.5 shard_map.73
  87.4 19.2 %all_to_all.35 = f32[32,1,6272]{2,1,0:T(1,128)S(1)} all-to-all(f32[32,1,6272]{2,1,0:T(1,128)S(1)} %bitcast.21), channel_id=1, replica_groups=mesh['af'=32,'vert'=8] {'af'}, dimensions={0} | all-to-all | bytes 1605632 | tf_op jit(solution)/shard_map/all_to_all | solution.py:318
  106.7 0.1 shard_map.74.mine
  106.8 9.9 %collective-permute-start = (f32[8,128]{1,0:T(8,128)S(1)}, f32[8,128]{1,0:T(8,128)S(1)}, u32[]{:S(2)}, u32[]{:S(2)}) collective-permute-start(f32[8,128]{1,0:T(8,128)S(1)} %shard_map.74.mine), channel_id=1, source_target_pairs={{0,1},{1,0},{2,3},{3,2},{4,5},{5,4},{6,7},{7,6},{8,9},{9,8},{10,11... | collective-permute-start | bytes 12296 | tf_op jit(solution)/shard_map/ppermute | solution.py:373
  116.7 0.8 collective-permute-done.other
  117.5 2.5 %collective-permute-start.3 = (f32[16,128]{1,0:T(8,128)S(1)}, f32[16,128]{1,0:T(8,128)S(1)}, u32[]{:S(2)}, u32[]{:S(2)}) collective-permute-start(f32[16,128]{1,0:T(8,128)S(1)} %shard_map.75.g0), channel_id=1, source_target_pairs={{0,6},{1,7},{2,4},{3,5},{4,2},{5,3},{6,0},{7,1},{8,14},{9,15},{10,... | collective-permute-start | bytes 24584 | tf_op jit(solution)/shard_map/ppermute | solution.py:374
  120.0 0.5 collective-permute-start.2
  120.5 0.3 collective-permute-start.1
  120.8 0.5 collective-permute-done.3.g3
  121.2 2.8 %collective-permute-done.2.g2 = f32[16,128]{1,0:T(8,128)S(1)} collective-permute-done((f32[16,128]{1,0:T(8,128)S(1)}, f32[16,128]{1,0:T(8,128)S(1)}, u32[]{:S(2)}, u32[]{:S(2)}) %collective-permute-start.2) | collective-permute-done | bytes 8224 | tf_op jit(solution)/shard_map/ppermute | solution.py:374
  124.0 0.0 collective-permute-done.1.g1
  124.0 1.1 shard_map.76
  (1 shorter events, 0.0 us)
Async XLA Ops:
  0.6 2.1 %copy-start.1 = (f32[8,8,192]{2,1,0:T(8,128)S(1)}, f32[8,8,192]{2,1,0:T(8,128)}, u32[]{:S(2)}) copy-start(f32[8,8,192]{2,1,0:T(8,128)} %q0_ref.1) | copy-start | bytes 147460
  2.7 22.2 %copy-start = (bf16[4,512,512]{2,1,0:T(8,128)(2,1)S(1)}, bf16[4,512,512]{2,1,0:T(8,128)(2,1)}, u32[]{:S(2)}) copy-start(bf16[4,512,512]{2,1,0:T(8,128)(2,1)} %constant.2.clone.refs_2_) | copy-start | bytes 6291460
  2.7 22.2 %copy-start.2 = (s32[512]{0:T(512)S(1)}, s32[512]{0:T(512)}, u32[]{:S(2)}) copy-start(s32[512]{0:T(512)} %param.6) | copy-start | bytes 6148
  106.8 10.7 %collective-permute-start = (f32[8,128]{1,0:T(8,128)S(1)}, f32[8,128]{1,0:T(8,128)S(1)}, u32[]{:S(2)}, u32[]{:S(2)}) collective-permute-start(f32[8,128]{1,0:T(8,128)S(1)} %shard_map.74.mine), channel_id=1, source_target_pairs={{0,1},{1,0},{2,3},{3,2},{4,5},{5,4},{6,7},{7,6},{8,9},{9,8},{10,11... | collective-permute-start | bytes 12296 | tf_op jit(solution)/shard_map/ppermute | solution.py:373
  117.5 3.7 %collective-permute-start.3 = (f32[16,128]{1,0:T(8,128)S(1)}, f32[16,128]{1,0:T(8,128)S(1)}, u32[]{:S(2)}, u32[]{:S(2)}) collective-permute-start(f32[16,128]{1,0:T(8,128)S(1)} %shard_map.75.g0), channel_id=1, source_target_pairs={{0,6},{1,7},{2,4},{3,5},{4,2},{5,3},{6,0},{7,1},{8,14},{9,15},{10,... | collective-permute-start | bytes 24584 | tf_op jit(solution)/shard_map/ppermute | solution.py:374
  120.0 4.0 %collective-permute-start.2 = (f32[16,128]{1,0:T(8,128)S(1)}, f32[16,128]{1,0:T(8,128)S(1)}, u32[]{:S(2)}, u32[]{:S(2)}) collective-permute-start(f32[16,128]{1,0:T(8,128)S(1)} %shard_map.75.g0), channel_id=1, source_target_pairs={{0,4},{1,5},{2,6},{3,7},{4,0},{5,1},{6,2},{7,3},{8,12},{9,13},{10,... | collective-permute-start | bytes 24584 | tf_op jit(solution)/shard_map/ppermute | solution.py:374
  120.5 3.5 %collective-permute-start.1 = (f32[16,128]{1,0:T(8,128)S(1)}, f32[16,128]{1,0:T(8,128)S(1)}, u32[]{:S(2)}, u32[]{:S(2)}) collective-permute-start(f32[16,128]{1,0:T(8,128)S(1)} %shard_map.75.g0), channel_id=1, source_target_pairs={{0,2},{1,3},{2,0},{3,1},{4,6},{5,7},{6,4},{7,5},{8,10},{9,11},{10,... | collective-permute-start | bytes 24584 | tf_op jit(solution)/shard_map/ppermute | solution.py:374

commit v8 on v7

--- a/solution.py
+++ b/solution.py
@@ -26,7 +26,7 @@
 MSG = KB + 1
 TB = SAMPLES // AF
 LAST = 3 * TB + 1
-CHUNKS = ((0, 2), (2, 2), (4, 2), (6, 2))
+CHUNKS = tuple((f, 1) for f in range(FB))
 
 
 def dft_tables():

time: 125 us -> 125 us (level)
  no operation moved by 1% of the time
where the time goes in v8:
time: 125 us
  blocking collectives  97.9 us (78%)
  starting transfers between devices  13.2 us (11%)
  Pallas kernels  9.13 us (7%)
  waiting for transfers between devices  4.06 us (3%)
    all_to_all x6, blocking collectives, exchange(): flat = lax.all_to_all(flat, 'af', split_axis=0, concat_axis=0, tiled=True)  97.9 us
    ppermute x1, starting transfers between devices, per_device(): lax.ppermute(stats, 'vert', [(i, i ^ 1) for i in range(VERT)])  9.92 us
    pallas_call x10, Pallas kernels, call(): pl.pallas_call(body, out_shape=[jax.ShapeDtypeStruct(s, t) for s, t in ou...  9.13 us
    ppermute x3, starting transfers between devices, per_device(): lax.ppermute(pair, 'vert', [(i, i ^ 2 * d) for i in range(VERT)])  3.25 us
    ppermute x3, waiting for transfers between devices, per_device(): lax.ppermute(pair, 'vert', [(i, i ^ 2 * d) for i in range(VERT)])  3.23 us
  transfers between devices with their start and end apart: 4, of which 3 were waited for; matrix products, arithmetic and copies ran while one was open for 0% of the time, Pallas kernels for 0%

profile of v8, /device:TPU:1, one launch (start us, length us, event | category | flops | bytes accessed | tf_op | source)
XLA Modules:
  0.0 125.0 jit_solution(3122543358168790719)
XLA Ops:
  0.6 0.0 copy-start.1
  0.6 2.0 %shard_map.67 = (bf16[8,192,512]{2,1,0:T(8,128)(2,1)S(1)}, bf16[8,192,512]{2,1,0:T(8,128)(2,1)S(1)}) custom-call(f32[8,192,512]{2,1,0:T(8,128)} %bitcast.30), custom_call_target="tpu_custom_call" | custom-call | tf_op jit(solution)/shard_map/pallas_call | solution.py:306
  2.6 0.0 copy-start
  2.6 0.0 copy-start.2
  2.7 0.0 copy-done.1
  2.7 0.7 shard_map.68
  3.4 21.5 %all_to_all.30 = f32[32,1,2048]{2,1,0:T(1,128)S(1)} all-to-all(f32[32,1,2048]{2,1,0:T(1,128)S(1)} %bitcast.26), channel_id=1, replica_groups=mesh['af'=32,'vert'=8] {'af'}, dimensions={0} | all-to-all | bytes 524288 | tf_op jit(solution)/shard_map/all_to_all | solution.py:318
  24.9 0.0 copy-done
  24.9 0.0 copy-done.2
  24.9 0.8 shard_map.69
  25.7 14.7 %all_to_all.31 = f32[32,1,2176]{2,1,0:T(1,128)S(1)} all-to-all(f32[32,1,2176]{2,1,0:T(1,128)S(1)} %bitcast.25), channel_id=1, replica_groups=mesh['af'=32,'vert'=8] {'af'}, dimensions={0} | all-to-all | bytes 557056 | tf_op jit(solution)/shard_map/all_to_all | solution.py:318
  40.4 1.6 %shard_map.70 = (f32[544,128]{1,0:T(8,128)S(1)}, f32[8,8,192]{2,1,0:T(8,128)S(1)}, f32[8,128]{1,0:T(8,128)S(1)}) custom-call(f32[544,128]{1,0:T(8,128)S(1)} %bitcast.18, bf16[8,192,512]{2,1,0:T(8,128)(2,1)S(1)} %get-tuple-element.22.khi_ref, bf16[8,192,512]{2,1,0:T(8,128)(2,1)S(1)} %get-tuple-element.23.klo_ref, ...), custom_call_target="tpu_custom_call" | custom-call | tf_op jit(solution)/shard_map/pallas_call | solution.py:306
  42.0 14.3 %all_to_all.32 = f32[32,1,2176]{2,1,0:T(1,128)S(1)} all-to-all(f32[32,1,2176]{2,1,0:T(1,128)S(1)} %bitcast.23), channel_id=1, replica_groups=mesh['af'=32,'vert'=8] {'af'}, dimensions={0} | all-to-all | bytes 557056 | tf_op jit(solution)/shard_map/all_to_all | solution.py:318
  56.3 0.8 shard_map.71
  57.2 14.1 %all_to_all.33 = f32[32,1,2176]{2,1,0:T(1,128)S(1)} all-to-all(f32[32,1,2176]{2,1,0:T(1,128)S(1)} %bitcast.24), channel_id=1, replica_groups=mesh['af'=32,'vert'=8] {'af'}, dimensions={0} | all-to-all | bytes 557056 | tf_op jit(solution)/shard_map/all_to_all | solution.py:318
  71.3 1.6 %shard_map.72 = (f32[544,128]{1,0:T(8,128)S(1)}, f32[8,8,192]{2,1,0:T(8,128)S(1)}, f32[8,128]{1,0:T(8,128)S(1)}) custom-call(f32[544,128]{1,0:T(8,128)S(1)} %bitcast.16, bf16[8,192,512]{2,1,0:T(8,128)(2,1)S(1)} %get-tuple-element.22.khi_ref, bf16[8,192,512]{2,1,0:T(8,128)(2,1)S(1)} %get-tuple-element.23.klo_ref, ...), custom_call_target="tpu_custom_call" | custom-call | tf_op jit(solution)/shard_map/pallas_call | solution.py:306
  72.8 14.1 %all_to_all.34 = f32[32,1,2176]{2,1,0:T(1,128)S(1)} all-to-all(f32[32,1,2176]{2,1,0:T(1,128)S(1)} %bitcast.22), channel_id=1, replica_groups=mesh['af'=32,'vert'=8] {'af'}, dimensions={0} | all-to-all | bytes 557056 | tf_op jit(solution)/shard_map/all_to_all | solution.py:318
  86.9 0.5 shard_map.73
  87.4 19.2 %all_to_all.35 = f32[32,1,6272]{2,1,0:T(1,128)S(1)} all-to-all(f32[32,1,6272]{2,1,0:T(1,128)S(1)} %bitcast.21), channel_id=1, replica_groups=mesh['af'=32,'vert'=8] {'af'}, dimensions={0} | all-to-all | bytes 1605632 | tf_op jit(solution)/shard_map/all_to_all | solution.py:318
  106.6 0.1 shard_map.74.mine
  106.7 9.9 %collective-permute-start = (f32[8,128]{1,0:T(8,128)S(1)}, f32[8,128]{1,0:T(8,128)S(1)}, u32[]{:S(2)}, u32[]{:S(2)}) collective-permute-start(f32[8,128]{1,0:T(8,128)S(1)} %shard_map.74.mine), channel_id=1, source_target_pairs={{0,1},{1,0},{2,3},{3,2},{4,5},{5,4},{6,7},{7,6},{8,9},{9,8},{10,11... | collective-permute-start | bytes 12296 | tf_op jit(solution)/shard_map/ppermute | solution.py:373
  116.7 0.8 collective-permute-done.other
  117.5 2.5 %collective-permute-start.3 = (f32[16,128]{1,0:T(8,128)S(1)}, f32[16,128]{1,0:T(8,128)S(1)}, u32[]{:S(2)}, u32[]{:S(2)}) collective-permute-start(f32[16,128]{1,0:T(8,128)S(1)} %shard_map.75.g0), channel_id=1, source_target_pairs={{0,6},{1,7},{2,4},{3,5},{4,2},{5,3},{6,0},{7,1},{8,14},{9,15},{10,... | collective-permute-start | bytes 24584 | tf_op jit(solution)/shard_map/ppermute | solution.py:374
  120.0 0.5 collective-permute-start.2
  120.5 0.3 collective-permute-start.1
  120.7 0.5 collective-permute-done.3.g3
  121.2 2.8 %collective-permute-done.2.g2 = f32[16,128]{1,0:T(8,128)S(1)} collective-permute-done((f32[16,128]{1,0:T(8,128)S(1)}, f32[16,128]{1,0:T(8,128)S(1)}, u32[]{:S(2)}, u32[]{:S(2)}) %collective-permute-start.2) | collective-permute-done | bytes 8224 | tf_op jit(solution)/shard_map/ppermute | solution.py:374
  124.0 0.0 collective-permute-done.1.g1
  124.0 1.1 shard_map.76
  (1 shorter events, 0.0 us)
Async XLA Ops:
  0.6 2.0 %copy-start.1 = (f32[8,8,192]{2,1,0:T(8,128)S(1)}, f32[8,8,192]{2,1,0:T(8,128)}, u32[]{:S(2)}) copy-start(f32[8,8,192]{2,1,0:T(8,128)} %q0_ref.1) | copy-start | bytes 147460
  2.6 22.2 %copy-start = (bf16[4,512,512]{2,1,0:T(8,128)(2,1)S(1)}, bf16[4,512,512]{2,1,0:T(8,128)(2,1)}, u32[]{:S(2)}) copy-start(bf16[4,512,512]{2,1,0:T(8,128)(2,1)} %constant.2.clone.refs_2_) | copy-start | bytes 6291460
  2.6 22.2 %copy-start.2 = (s32[512]{0:T(512)S(1)}, s32[512]{0:T(512)}, u32[]{:S(2)}) copy-start(s32[512]{0:T(512)} %param.6) | copy-start | bytes 6148
  106.7 10.7 %collective-permute-start = (f32[8,128]{1,0:T(8,128)S(1)}, f32[8,128]{1,0:T(8,128)S(1)}, u32[]{:S(2)}, u32[]{:S(2)}) collective-permute-start(f32[8,128]{1,0:T(8,128)S(1)} %shard_map.74.mine), channel_id=1, source_target_pairs={{0,1},{1,0},{2,3},{3,2},{4,5},{5,4},{6,7},{7,6},{8,9},{9,8},{10,11... | collective-permute-start | bytes 12296 | tf_op jit(solution)/shard_map/ppermute | solution.py:373
  117.5 3.7 %collective-permute-start.3 = (f32[16,128]{1,0:T(8,128)S(1)}, f32[16,128]{1,0:T(8,128)S(1)}, u32[]{:S(2)}, u32[]{:S(2)}) collective-permute-start(f32[16,128]{1,0:T(8,128)S(1)} %shard_map.75.g0), channel_id=1, source_target_pairs={{0,6},{1,7},{2,4},{3,5},{4,2},{5,3},{6,0},{7,1},{8,14},{9,15},{10,... | collective-permute-start | bytes 24584 | tf_op jit(solution)/shard_map/ppermute | solution.py:374
  120.0 4.0 %collective-permute-start.2 = (f32[16,128]{1,0:T(8,128)S(1)}, f32[16,128]{1,0:T(8,128)S(1)}, u32[]{:S(2)}, u32[]{:S(2)}) collective-permute-start(f32[16,128]{1,0:T(8,128)S(1)} %shard_map.75.g0), channel_id=1, source_target_pairs={{0,4},{1,5},{2,6},{3,7},{4,0},{5,1},{6,2},{7,3},{8,12},{9,13},{10,... | collective-permute-start | bytes 24584 | tf_op jit(solution)/shard_map/ppermute | solution.py:374
  120.5 3.5 %collective-permute-start.1 = (f32[16,128]{1,0:T(8,128)S(1)}, f32[16,128]{1,0:T(8,128)S(1)}, u32[]{:S(2)}, u32[]{:S(2)}) collective-permute-start(f32[16,128]{1,0:T(8,128)S(1)} %shard_map.75.g0), channel_id=1, source_target_pairs={{0,2},{1,3},{2,0},{3,1},{4,6},{5,7},{6,4},{7,5},{8,10},{9,11},{10,... | collective-permute-start | bytes 24584 | tf_op jit(solution)/shard_map/ppermute | solution.py:374

commit v9 on v8

--- a/solution.py
+++ b/solution.py
@@ -239,7 +239,7 @@
     out[pl.ds(8, 8), :] = other[...]
 
 
-def last_kernel(recv, g0, g1, g2, g3, q0_ref, q1_ref, q2_ref, sol_ref, dir_ref, left_ref, rows):
+def last_kernel(recv, g0, g1, g2, g3, q0_ref, q1_ref, q2_ref, sol_out, dir_out, left_out, rows, sol_ref, dir_ref, left_ref, sems):
     gathered = (g0, g1, g2, g3)
     n0, m1, n1, m2, n2, m3 = [
         jnp.concatenate([g[pl.ds(8 * c + j, 1), :] for g in gathered for c in range(2)], axis=0)
@@ -296,13 +296,23 @@
             s1, s2, s3 = [recv[pl.ds(at + j * TB, TB), :] for j in range(3)]
             sol_ref[v, :, q * 128 : (q + 1) * 128] = x1 * s1 + x2 * s2
             dir_ref[v, :, q * 128 : (q + 1) * 128] = y1 * s1 + y2 * s2 + y3 * s3
+    copies = [
+        pltpu.make_async_copy(sol_ref, sol_out, sems.at[0]),
+        pltpu.make_async_copy(dir_ref, dir_out, sems.at[1]),
+    ]
+    for copy in copies:
+        copy.start()
     c0, c1, c2 = c0[:, :1], c1[:, :1], c2[:, :1]
     for f in range(FB):
         left_ref[f] = c0 * q0_ref[f] + c1 * q1_ref[f] + c2 * q2_ref[f]
-
-
-def call(body, outs, *operands, scratch=(), space=pltpu.VMEM, vmem=16):
-    here = pl.BlockSpec(memory_space=pltpu.VMEM)
+    copies.append(pltpu.make_async_copy(left_ref, left_out, sems.at[2]))
+    copies[-1].start()
+    for copy in copies:
+        copy.wait()
+
+
+def call(body, outs, *operands, scratch=(), space=pltpu.VMEM, vmem=16, to=pltpu.VMEM):
+    here = pl.BlockSpec(memory_space=to)
     return pl.pallas_call(
         body,
         out_shape=[jax.ShapeDtypeStruct(s, t) for s, t in outs],
@@ -378,7 +388,10 @@
             last_kernel,
             [out, out, data],
             arrived, *gathered, recorded, q1, q2,
-            scratch=[pltpu.VMEM((64, 128), F32)],
+            scratch=[pltpu.VMEM((64, 128), F32)]
+            + [pltpu.VMEM(*o) for o in (out, out, data)]
+            + [pltpu.SemaphoreType.DMA((3,))],
+            to=pltpu.HBM,
         )
     )
 

time: 125 us -> 125 us (level)
  no operation moved by 1% of the time
where the time goes in v9:
time: 125 us
  blocking collectives  97.9 us (78%)
  starting transfers between devices  13.2 us (11%)
  Pallas kernels  9.15 us (7%)
  waiting for transfers between devices  4.06 us (3%)
    all_to_all x6, blocking collectives, exchange(): flat = lax.all_to_all(flat, 'af', split_axis=0, concat_axis=0, tiled=True)  97.9 us
    ppermute x1, starting transfers between devices, per_device(): lax.ppermute(stats, 'vert', [(i, i ^ 1) for i in range(VERT)])  9.92 us
    pallas_call x10, Pallas kernels, call(): pl.pallas_call(body, out_shape=[jax.ShapeDtypeStruct(s, t) for s, t in ou...  9.15 us
    ppermute x3, starting transfers between devices, per_device(): lax.ppermute(pair, 'vert', [(i, i ^ 2 * d) for i in range(VERT)])  3.25 us
    ppermute x3, waiting for transfers between devices, per_device(): lax.ppermute(pair, 'vert', [(i, i ^ 2 * d) for i in range(VERT)])  3.23 us
  transfers between devices with their start and end apart: 4, of which 3 were waited for; matrix products, arithmetic and copies ran while one was open for 0% of the time, Pallas kernels for 0%

profile of v9, /device:TPU:1, one launch (start us, length us, event | category | flops | bytes accessed | tf_op | source)
XLA Modules:
  0.0 125.0 jit_solution(8554437114823126560)
XLA Ops:
  0.6 0.0 copy-start.1
  0.6 2.0 %shard_map.67 = (bf16[8,192,512]{2,1,0:T(8,128)(2,1)S(1)}, bf16[8,192,512]{2,1,0:T(8,128)(2,1)S(1)}) custom-call(f32[8,192,512]{2,1,0:T(8,128)} %bitcast.30), custom_call_target="tpu_custom_call" | custom-call | tf_op jit(solution)/shard_map/pallas_call | solution.py:316
  2.6 0.0 copy-start
  2.6 0.0 copy-start.2
  2.7 0.0 copy-done.1
  2.7 0.7 shard_map.68
  3.4 21.5 %all_to_all.30 = f32[32,1,2048]{2,1,0:T(1,128)S(1)} all-to-all(f32[32,1,2048]{2,1,0:T(1,128)S(1)} %bitcast.26), channel_id=1, replica_groups=mesh['af'=32,'vert'=8] {'af'}, dimensions={0} | all-to-all | bytes 524288 | tf_op jit(solution)/shard_map/all_to_all | solution.py:328
  24.9 0.0 copy-done
  24.9 0.0 copy-done.2
  24.9 0.8 shard_map.69
  25.7 14.7 %all_to_all.31 = f32[32,1,2176]{2,1,0:T(1,128)S(1)} all-to-all(f32[32,1,2176]{2,1,0:T(1,128)S(1)} %bitcast.25), channel_id=1, replica_groups=mesh['af'=32,'vert'=8] {'af'}, dimensions={0} | all-to-all | bytes 557056 | tf_op jit(solution)/shard_map/all_to_all | solution.py:328
  40.4 1.6 %shard_map.70 = (f32[544,128]{1,0:T(8,128)S(1)}, f32[8,8,192]{2,1,0:T(8,128)S(1)}, f32[8,128]{1,0:T(8,128)S(1)}) custom-call(f32[544,128]{1,0:T(8,128)S(1)} %bitcast.18, bf16[8,192,512]{2,1,0:T(8,128)(2,1)S(1)} %get-tuple-element.22.khi_ref, bf16[8,192,512]{2,1,0:T(8,128)(2,1)S(1)} %get-tuple-element.23.klo_ref, ...), custom_call_target="tpu_custom_call" | custom-call | tf_op jit(solution)/shard_map/pallas_call | solution.py:316
  42.0 14.3 %all_to_all.32 = f32[32,1,2176]{2,1,0:T(1,128)S(1)} all-to-all(f32[32,1,2176]{2,1,0:T(1,128)S(1)} %bitcast.23), channel_id=1, replica_groups=mesh['af'=32,'vert'=8] {'af'}, dimensions={0} | all-to-all | bytes 557056 | tf_op jit(solution)/shard_map/all_to_all | solution.py:328
  56.3 0.8 shard_map.71
  57.2 14.1 %all_to_all.33 = f32[32,1,2176]{2,1,0:T(1,128)S(1)} all-to-all(f32[32,1,2176]{2,1,0:T(1,128)S(1)} %bitcast.24), channel_id=1, replica_groups=mesh['af'=32,'vert'=8] {'af'}, dimensions={0} | all-to-all | bytes 557056 | tf_op jit(solution)/shard_map/all_to_all | solution.py:328
  71.3 1.6 %shard_map.72 = (f32[544,128]{1,0:T(8,128)S(1)}, f32[8,8,192]{2,1,0:T(8,128)S(1)}, f32[8,128]{1,0:T(8,128)S(1)}) custom-call(f32[544,128]{1,0:T(8,128)S(1)} %bitcast.16, bf16[8,192,512]{2,1,0:T(8,128)(2,1)S(1)} %get-tuple-element.22.khi_ref, bf16[8,192,512]{2,1,0:T(8,128)(2,1)S(1)} %get-tuple-element.23.klo_ref, ...), custom_call_target="tpu_custom_call" | custom-call | tf_op jit(solution)/shard_map/pallas_call | solution.py:316
  72.8 14.1 %all_to_all.34 = f32[32,1,2176]{2,1,0:T(1,128)S(1)} all-to-all(f32[32,1,2176]{2,1,0:T(1,128)S(1)} %bitcast.22), channel_id=1, replica_groups=mesh['af'=32,'vert'=8] {'af'}, dimensions={0} | all-to-all | bytes 557056 | tf_op jit(solution)/shard_map/all_to_all | solution.py:328
  86.9 0.5 shard_map.73
  87.4 19.2 %all_to_all.35 = f32[32,1,6272]{2,1,0:T(1,128)S(1)} all-to-all(f32[32,1,6272]{2,1,0:T(1,128)S(1)} %bitcast.21), channel_id=1, replica_groups=mesh['af'=32,'vert'=8] {'af'}, dimensions={0} | all-to-all | bytes 1605632 | tf_op jit(solution)/shard_map/all_to_all | solution.py:328
  106.6 0.1 shard_map.74.mine
  106.7 9.9 %collective-permute-start = (f32[8,128]{1,0:T(8,128)S(1)}, f32[8,128]{1,0:T(8,128)S(1)}, u32[]{:S(2)}, u32[]{:S(2)}) collective-permute-start(f32[8,128]{1,0:T(8,128)S(1)} %shard_map.74.mine), channel_id=1, source_target_pairs={{0,1},{1,0},{2,3},{3,2},{4,5},{5,4},{6,7},{7,6},{8,9},{9,8},{10,11... | collective-permute-start | bytes 12296 | tf_op jit(solution)/shard_map/ppermute | solution.py:383
  116.7 0.8 collective-permute-done.other
  117.5 2.5 %collective-permute-start.3 = (f32[16,128]{1,0:T(8,128)S(1)}, f32[16,128]{1,0:T(8,128)S(1)}, u32[]{:S(2)}, u32[]{:S(2)}) collective-permute-start(f32[16,128]{1,0:T(8,128)S(1)} %shard_map.75.g0), channel_id=1, source_target_pairs={{0,6},{1,7},{2,4},{3,5},{4,2},{5,3},{6,0},{7,1},{8,14},{9,15},{10,... | collective-permute-start | bytes 24584 | tf_op jit(solution)/shard_map/ppermute | solution.py:384
  120.0 0.5 collective-permute-start.2
  120.5 0.3 collective-permute-start.1
  120.7 0.5 collective-permute-done.3.g3
  121.2 2.8 %collective-permute-done.2.g2 = f32[16,128]{1,0:T(8,128)S(1)} collective-permute-done((f32[16,128]{1,0:T(8,128)S(1)}, f32[16,128]{1,0:T(8,128)S(1)}, u32[]{:S(2)}, u32[]{:S(2)}) %collective-permute-start.2) | collective-permute-done | bytes 8224 | tf_op jit(solution)/shard_map/ppermute | solution.py:384
  124.0 0.0 collective-permute-done.1.g1
  124.0 1.1 shard_map.76
  (1 shorter events, 0.0 us)
Async XLA Ops:
  0.6 2.0 %copy-start.1 = (f32[8,8,192]{2,1,0:T(8,128)S(1)}, f32[8,8,192]{2,1,0:T(8,128)}, u32[]{:S(2)}) copy-start(f32[8,8,192]{2,1,0:T(8,128)} %q0_ref.1) | copy-start | bytes 147460
  2.6 22.2 %copy-start = (bf16[4,512,512]{2,1,0:T(8,128)(2,1)S(1)}, bf16[4,512,512]{2,1,0:T(8,128)(2,1)}, u32[]{:S(2)}) copy-start(bf16[4,512,512]{2,1,0:T(8,128)(2,1)} %constant.2.clone.refs_2_) | copy-start | bytes 6291460
  2.6 22.2 %copy-start.2 = (s32[512]{0:T(512)S(1)}, s32[512]{0:T(512)}, u32[]{:S(2)}) copy-start(s32[512]{0:T(512)} %param.6) | copy-start | bytes 6148
  106.7 10.7 %collective-permute-start = (f32[8,128]{1,0:T(8,128)S(1)}, f32[8,128]{1,0:T(8,128)S(1)}, u32[]{:S(2)}, u32[]{:S(2)}) collective-permute-start(f32[8,128]{1,0:T(8,128)S(1)} %shard_map.74.mine), channel_id=1, source_target_pairs={{0,1},{1,0},{2,3},{3,2},{4,5},{5,4},{6,7},{7,6},{8,9},{9,8},{10,11... | collective-permute-start | bytes 12296 | tf_op jit(solution)/shard_map/ppermute | solution.py:383
  117.5 3.7 %collective-permute-start.3 = (f32[16,128]{1,0:T(8,128)S(1)}, f32[16,128]{1,0:T(8,128)S(1)}, u32[]{:S(2)}, u32[]{:S(2)}) collective-permute-start(f32[16,128]{1,0:T(8,128)S(1)} %shard_map.75.g0), channel_id=1, source_target_pairs={{0,6},{1,7},{2,4},{3,5},{4,2},{5,3},{6,0},{7,1},{8,14},{9,15},{10,... | collective-permute-start | bytes 24584 | tf_op jit(solution)/shard_map/ppermute | solution.py:384
  120.0 4.0 %collective-permute-start.2 = (f32[16,128]{1,0:T(8,128)S(1)}, f32[16,128]{1,0:T(8,128)S(1)}, u32[]{:S(2)}, u32[]{:S(2)}) collective-permute-start(f32[16,128]{1,0:T(8,128)S(1)} %shard_map.75.g0), channel_id=1, source_target_pairs={{0,4},{1,5},{2,6},{3,7},{4,0},{5,1},{6,2},{7,3},{8,12},{9,13},{10,... | collective-permute-start | bytes 24584 | tf_op jit(solution)/shard_map/ppermute | solution.py:384
  120.5 3.5 %collective-permute-start.1 = (f32[16,128]{1,0:T(8,128)S(1)}, f32[16,128]{1,0:T(8,128)S(1)}, u32[]{:S(2)}, u32[]{:S(2)}) collective-permute-start(f32[16,128]{1,0:T(8,128)S(1)} %shard_map.75.g0), channel_id=1, source_target_pairs={{0,2},{1,3},{2,0},{3,1},{4,6},{5,7},{6,4},{7,5},{8,10},{9,11},{10,... | collective-permute-start | bytes 24584 | tf_op jit(solution)/shard_map/ppermute | solution.py:384
